TPU v7x, 128 devices: a whole 4x4x4 slice. The times are simulated.
128 devices in a mesh: blk: 4 (over z), grp: 32 (over x, y, core).
Axes of the slice: x: 4, y: 4, z: 4, core: 2. Of those that a mesh axis runs over, the one named last changes fastest.
Arguments:
- loads: float32 [524288, 256], P(('blk', 'grp')), may hold values from -45 to 45
- pore_diag: float32 [524288], P(('blk', 'grp')), may hold values from 2 to 8
- near_blocks: float32 [12288, 128, 128], P(('blk', 'grp')), may hold values from -0.125 to 0.125
- near_cols: int32 [12288], P(('blk', 'grp')), may hold values from 0 to 39
- short_blocks: float32 [512, 2, 128, 128], P(('blk', 'grp')), may hold values from -0.125 to 0.125
- short_rows: int32 [512, 2], P(('blk', 'grp')), may hold values from 0 to 31
- short_cols: int32 [512, 2], P(('blk', 'grp')), may hold values from 0 to 31
Outputs:
- solution: float32 [524288, 256], P(('blk', 'grp'))
- residual: float32 [524288, 256], P(('blk', 'grp'))
All inputs are finite; a program needn't handle non-finite values.
Results may differ from a plain program's by a relative error of at most 0.0003.
Values sent between devices are 32-bit elements; how exact they have to be, the bound alone decides.
A program may use at most 192 MiB of HBM per device.

v0:
```python
import jax
import jax.numpy as jnp
from jax import lax
from jax.sharding import PartitionSpec as P

NEAR_PER = 3
HB = 4


HIGH = lax.Precision.HIGHEST


def with_halo(block, sides, width):
    for axis, dim in sides:
        count = lax.axis_size(axis)
        forward = [(i, i + 1) for i in range(count - 1)]
        forward.append((count - 1, 0))
        backward = [(target, source) for source, target in forward]
        low = lax.ppermute(
            lax.slice_in_dim(block, block.shape[dim] - width, None, axis=dim), axis, forward
        )
        high = lax.ppermute(lax.slice_in_dim(block, 0, width, axis=dim), axis, backward)
        block = jnp.concatenate([low, block, high], axis=dim)
    return block


def chol_solve(matrix, rhs):
    factor = jnp.linalg.cholesky(matrix)
    middle = lax.linalg.triangular_solve(factor, rhs, left_side=True, lower=True)
    return lax.linalg.triangular_solve(factor, middle, left_side=True, lower=True, transpose_a=True)


def inner(left, right):
    return jnp.einsum("nc,nd->cd", left, right, precision=HIGH)


def one_hot(indices, count):
    return (indices[:, None] == jnp.arange(count, dtype=jnp.int32)[None, :]).astype(jnp.float32)


def spread_rows(selector, terms):
    return jnp.einsum("kq,kan->qan", selector, terms, precision=HIGH)


def body(loads, pore_diag, near_blocks, near_cols, short_blocks, short_rows, short_cols):
    total_rows, cases = loads.shape
    block = near_blocks.shape[1]
    brows = total_rows // block
    near_mats = near_blocks.reshape(brows, NEAR_PER, block, block)
    near_select = one_hot(near_cols, brows + 2 * HB)
    row_select = one_hot(short_rows.reshape(-1), brows)
    wanted = lax.all_to_all(short_cols, "blk", split_axis=0, concat_axis=0, tiled=True)
    wanted_select = one_hot(wanted.reshape(-1), brows)

    def shortcut(slab_blocks):
        fetch = slab_blocks[wanted]
        mine = slab_blocks[short_rows]
        sent_terms = jnp.einsum("csji,csjn->csin", short_blocks, mine, precision=HIGH)
        got_rows, got_terms = (
            lax.all_to_all(fetch, "blk", split_axis=0, concat_axis=0, tiled=True),
            lax.all_to_all(sent_terms, "blk", split_axis=0, concat_axis=0, tiled=True),
        )
        reach = jnp.einsum("csij,csjn->csin", short_blocks, got_rows, precision=HIGH)
        placed = spread_rows(row_select, reach.reshape(-1, block, cases))
        return placed + spread_rows(wanted_select, got_terms.reshape(-1, block, cases))

    def operate(field):
        slab_blocks = field.reshape(brows, block, cases)
        backward = jnp.einsum("rjba,rbn->rjan", near_mats, slab_blocks, precision=HIGH)
        placed = spread_rows(near_select, backward.reshape(brows * NEAR_PER, block, cases))
        extended = with_halo(slab_blocks, (("grp", 0),), HB)
        rim_parts = jnp.concatenate([placed[:HB], placed[HB + brows :]], axis=0)
        rim_in = with_halo(rim_parts, (("grp", 0),), HB)
        rim_front = rim_in[:HB]
        rim_back = rim_in[3 * HB :]
        partner = extended[near_cols].reshape(brows, NEAR_PER, block, cases)
        forward = jnp.einsum("rjab,rjbn->ran", near_mats, partner, precision=HIGH)
        own = forward + placed[HB : HB + brows]
        own = own.at[:HB].add(rim_front)
        own = own.at[brows - HB :].add(rim_back)
        own = own + shortcut(slab_blocks)
        return pore_diag[:, None] * field + own.reshape(total_rows, cases)

    def summed(local):
        return lax.psum(local, ("blk", "grp"))

    rr_zero = summed(inner(loads, loads))
    image_one = operate(loads)
    gram_one = summed(inner(loads, image_one))
    pq_one = 0.5 * (gram_one + gram_one.T)
    alpha_one = chol_solve(pq_one, rr_zero)
    sol_one = jnp.dot(loads, alpha_one, precision=HIGH)
    resid_one = loads - jnp.dot(image_one, alpha_one, precision=HIGH)
    rr_one = summed(inner(resid_one, resid_one))
    beta_one = chol_solve(rr_zero, rr_one)
    search_one = resid_one + jnp.dot(loads, beta_one, precision=HIGH)
    image_two = operate(search_one)
    gram_two = summed(inner(search_one, image_two))
    pq_two = 0.5 * (gram_two + gram_two.T)
    alpha_two = chol_solve(pq_two, rr_one)
    solution = sol_one + jnp.dot(search_one, alpha_two, precision=HIGH)
    residual = resid_one - jnp.dot(image_two, alpha_two, precision=HIGH)
    return (solution, residual)


def solution(mesh):
    in_specs = (
        P(("blk", "grp"), None),
        P(("blk", "grp")),
        P(("blk", "grp"), None, None),
        P(("blk", "grp")),
        P(("blk", "grp"), None, None, None),
        P(("blk", "grp"), None),
        P(("blk", "grp"), None),
    )
    out_specs = (P(("blk", "grp"), None), P(("blk", "grp"), None))
    return jax.shard_map(body, mesh=mesh, in_specs=in_specs, out_specs=out_specs, check_vma=False)
```

profile of v0, /device:TPU:1, one launch (start us, length us, event | category | flops | bytes accessed | tf_op | source)
XLA Modules:
  0.0 905.4 jit_solution(5733201400080048648)
XLA Ops:
  12.2 14.1 %fusion.79 = f32[32,3,128,256]{3,2,1,0:T(8,128)S(1)} fusion(f32[32,3,128,128]{3,2,1,0:T(8,128)} %bitcast.251, f32[32,128,256,1]{2,1,3,0:T(8,128)} %bitcast.243), kind=kOutput, calls=%fused_computation.164 | convolution fusion | flops 4831838208 | bytes 23068672 | tf_op jit(solution)/shard_map/rjba,rbn->rjan/dot_general | solution.py:69
  26.3 12.6 %fusion = f32[40,128,256]{2,0,1:T(8,128)S(1)} fusion(f32[96,128,256]{2,1,0:T(8,128)S(1)} %bitcast.255, s32[96]{0:T(128)S(1)} %copy-done.16), kind=kOutput, calls=%fused_computation.12 | convolution fusion | flops 1509953280 | bytes 17826176 | tf_op jit(solution)/shard_map/kq,kan->qan/dot_general | solution.py:42
  47.3 5.0 all-to-all-start
  52.4 11.0 %fusion.81 = f32[256,256]{0,1:T(8,128)} fusion(f32[4096,256]{1,0:T(8,128)} %param.20), kind=kOutput, calls=%fused_computation.166 | convolution fusion | flops 3221225472 | bytes 4456448 | tf_op jit(solution)/shard_map/nc,nd->cd/dot_general | solution.py:34
  69.3 5.3 slice.301
  74.7 4.7 all-to-all-start.2
  85.2 5.3 pad_maximum_fusion
  90.5 11.2 %gather_fusion = f32[96,128,256]{2,1,0:T(8,128)} fusion(f32[40,128,256]{2,1,0:T(8,128)} %pad_maximum_fusion, s32[1024]{0:T(1024)S(1)} %pad_clamp_fusion.2), kind=kCustom, calls=%fused_computation | custom fusion | bytes 25166208 | tf_op jit(solution)/shard_map/gather | solution.py:76
  101.7 16.8 %copy_add_fusion.1 = f32[32,128,256]{2,1,0:T(8,128)} fusion(f32[32,128,256]{2,0,1:T(8,128)} %slice.301, f32[32,3,128,256]{3,2,1,0:T(8,128)} %bitcast.258, f32[32,3,128,128]{3,2,1,0:T(8,128)} %bitcast.252), kind=kOutput, calls=%fused_computation.23 | convolution fusion | flops 4832886784 | bytes 27262976 | tf_op jit(solution)/shard_map/rjab,rjbn->ran/dot_general | solution.py:77
  118.5 4.2 all-to-all-start.1
  128.3 5.1 fusion.61
  137.1 7.1 fusion.4
  147.6 7.8 convolution_bitcast_fusion.4
  155.8 149.1 %all-reduce.10.cloned.1.call-done = (f32[256,256]{0,1:T(8,128)}, f32[256,256]{1,0:T(8,128)}) async-done(((f32[256,256]{0,1:T(8,128)}, f32[256,256]{1,0:T(8,128)}), (f32[256,256]{0,1:T(8,128)}, f32[256,256]{1,0:T(8,128)})) %all-reduce.10.cloned.1.call-update) | async-done | bytes 524304 | tf_op jit(solution)/shard_map/psum | solution.py:85
  307.3 11.7 %cholesky.172 = f32[128,128]{1,0:T(8,128)S(1)} custom-call(f32[128,128]{1,0:T(8,128)S(1)} %cholesky.270), custom_call_target="Cholesky" | custom-call | tf_op jit(solution)/shard_map/jit(cholesky)/cholesky | solution.py:28
  319.1 9.8 %custom-call.20 = f32[1,128,128]{1,2,0:T(8,128)S(1)} custom-call(f32[1,128,128]{2,1,0:T(8,128)S(1)} %get-tuple-element.156), custom_call_target="InvertDiagBlocksLowerTriangular" | custom-call | tf_op jit(solution)/shard_map/jit(cholesky)/cholesky | solution.py:28
  329.4 11.7 %cholesky.189 = f32[128,128]{1,0:T(8,128)S(1)} custom-call(f32[128,128]{1,0:T(8,128)S(1)} %convolution_subtract_fusion.10), custom_call_target="Cholesky" | custom-call | tf_op jit(solution)/shard_map/jit(cholesky)/cholesky | solution.py:28
  343.1 3.9 while.16
  347.0 19.8 %custom-call.22 = f32[2,128,128]{1,2,0:T(8,128)S(1)} custom-call(f32[2,128,128]{2,1,0:T(8,128)S(1)} %get-tuple-element.94), custom_call_target="InvertDiagBlocksLowerTriangular" | custom-call | tf_op jit(solution)/shard_map/triangular_solve/custom-call.4 | solution.py:30
  368.9 6.9 convolution_subtract_fusion.1
  377.8 7.5 fusion.82
  385.3 11.9 %cholesky.206 = f32[128,128]{1,0:T(8,128)S(1)} custom-call(f32[128,128]{1,0:T(8,128)S(1)} %cholesky.273), custom_call_target="Cholesky" | custom-call | tf_op jit(solution)/shard_map/jit(cholesky)/cholesky | solution.py:28
  397.3 9.8 %custom-call.23 = f32[1,128,128]{1,2,0:T(8,128)S(1)} custom-call(f32[1,128,128]{2,1,0:T(8,128)S(1)} %get-tuple-element.152), custom_call_target="InvertDiagBlocksLowerTriangular" | custom-call | tf_op jit(solution)/shard_map/jit(cholesky)/cholesky | solution.py:28
  407.6 11.7 %cholesky.223 = f32[128,128]{1,0:T(8,128)S(1)} custom-call(f32[128,128]{1,0:T(8,128)S(1)} %convolution_subtract_fusion.9), custom_call_target="Cholesky" | custom-call | tf_op jit(solution)/shard_map/jit(cholesky)/cholesky | solution.py:28
  421.3 3.8 while.17
  425.1 20.1 %custom-call.25 = f32[2,128,128]{1,2,0:T(8,128)S(1)} custom-call(f32[2,128,128]{2,1,0:T(8,128)S(1)} %get-tuple-element.96), custom_call_target="InvertDiagBlocksLowerTriangular" | custom-call | tf_op jit(solution)/shard_map/triangular_solve/custom-call.4 | solution.py:30
  445.2 81.0 %all-reduce.6.cloned.1.call-done = f32[256,256]{1,0:T(8,128)} async-done(((f32[256,256]{1,0:T(8,128)}), f32[256,256]{1,0:T(8,128)}) %all-reduce.6.cloned.1.call-update) | async-done | bytes 262160 | tf_op jit(solution)/shard_map/psum | solution.py:85
  529.7 6.9 fusion.2
  545.3 16.0 %fusion.83 = f32[32,256,3,128]{3,1,2,0:T(8,128)} fusion(f32[32,128,256,1]{2,1,3,0:T(8,128)} %bitcast.249, f32[32,3,128,128]{3,2,1,0:T(8,128)} %bitcast.253), kind=kOutput, calls=%fused_computation.168 | convolution fusion | flops 4831838208 | bytes 23068672 | tf_op jit(solution)/shard_map/rjba,rbn->rjan/dot_general | solution.py:69
  561.3 12.7 %copy.105 = f32[96,128,256]{2,0,1:T(8,128)} copy(f32[96,128,256]{1,2,0:T(8,128)} %bitcast.256) | data formatting | bytes 25165824 | tf_op jit(solution)/shard_map/reshape | solution.py:70
  574.0 8.1 fusion.48
  597.8 5.3 pad_maximum_fusion.1
  603.1 11.2 %gather_fusion.3 = f32[96,128,256]{2,1,0:T(8,128)} fusion(f32[40,128,256]{2,1,0:T(8,128)} %pad_maximum_fusion.1, s32[1024]{0:T(1024)S(1)} %pad_clamp_fusion.2), kind=kCustom, calls=%fused_computation.3 | custom fusion | bytes 25166208 | tf_op jit(solution)/shard_map/gather | solution.py:76
  614.3 16.8 %copy_add_fusion = f32[32,128,256]{2,1,0:T(8,128)} fusion(f32[32,128,256]{2,0,1:T(8,128)} %slice.318, f32[32,3,128,256]{3,2,1,0:T(8,128)} %bitcast.257, f32[32,3,128,128]{3,2,1,0:T(8,128)} %bitcast.254), kind=kOutput, calls=%fused_computation.22 | convolution fusion | flops 4832886784 | bytes 27262976 | tf_op jit(solution)/shard_map/rjab,rjbn->ran/dot_general | solution.py:77
  631.1 4.2 all-to-all-start.3
  641.1 5.1 fusion.59
  650.0 7.1 fusion.3
  660.3 7.8 fusion.85
  668.1 12.8 %convolution_bitcast_fusion.1 = f32[4096,256]{0,1:T(8,128)} fusion(f32[4096,256]{1,0:T(8,128)} %param.20, f32[128,256]{1,0:T(8,128)S(1)} %fusion.34, f32[128,256]{1,0:T(8,128)S(1)} %fusion.32), kind=kOutput, calls=%fused_computation.19 | convolution fusion | flops 3221291008 | bytes 8650752 | tf_op jit(solution)/shard_map/dot_general | solution.py:92
  680.9 132.6 %all-reduce.8.cloned.1.call-done = f32[256,256]{1,0:T(8,128)} async-done(((f32[256,256]{1,0:T(8,128)}), f32[256,256]{1,0:T(8,128)}) %all-reduce.8.cloned.1.call-update) | async-done | bytes 262160 | tf_op jit(solution)/shard_map/psum | solution.py:85
  815.8 11.7 %cholesky.240 = f32[128,128]{1,0:T(8,128)S(1)} custom-call(f32[128,128]{1,0:T(8,128)S(1)} %cholesky.276), custom_call_target="Cholesky" | custom-call | tf_op jit(solution)/shard_map/jit(cholesky)/cholesky | solution.py:28
  827.6 9.8 %custom-call.26 = f32[1,128,128]{1,2,0:T(8,128)S(1)} custom-call(f32[1,128,128]{2,1,0:T(8,128)S(1)} %get-tuple-element.148), custom_call_target="InvertDiagBlocksLowerTriangular" | custom-call | tf_op jit(solution)/shard_map/jit(cholesky)/cholesky | solution.py:28
  837.9 11.7 %cholesky.257 = f32[128,128]{1,0:T(8,128)S(1)} custom-call(f32[128,128]{1,0:T(8,128)S(1)} %convolution_subtract_fusion.8), custom_call_target="Cholesky" | custom-call | tf_op jit(solution)/shard_map/jit(cholesky)/cholesky | solution.py:28
  852.4 4.2 while.18
  856.6 19.9 %custom-call.28 = f32[2,128,128]{1,2,0:T(8,128)S(1)} custom-call(f32[2,128,128]{2,1,0:T(8,128)S(1)} %get-tuple-element.98), custom_call_target="InvertDiagBlocksLowerTriangular" | custom-call | tf_op jit(solution)/shard_map/triangular_solve/custom-call.4 | solution.py:30
  878.4 9.0 convolution_subtract_fusion
  887.4 5.4 convolution_add_fusion
  892.8 5.6 copy.118
  (188 shorter events, 105.4 us)
Async XLA Ops:
  7.2 59.2 %copy-start = (f32[4,2,128,128]{3,2,1,0:T(8,128)S(1)}, f32[4,2,128,128]{3,2,1,0:T(8,128)}, u32[]{:S(2)}) copy-start(f32[4,2,128,128]{3,2,1,0:T(8,128)} %param.24) | copy-start | bytes 1572868
  9.5 75.7 %collective-permute-start.1 = (f32[4,128,256]{2,1,0:T(8,128)}, f32[4,128,256]{2,1,0:T(8,128)}, u32[]{:S(2)}, u32[]{:S(2)}) collective-permute-start(f32[4,128,256]{2,1,0:T(8,128)} %bitcast.2), channel_id=1, source_target_pairs={{1,0},{2,1},{3,2},{4,3},{5,4},{6,5},{7,6},{8,7},{9,8},{10,9},{11,1... | collective-permute-start | bytes 1572872 | tf_op jit(solution)/shard_map/ppermute | solution.py:22
  10.9 74.3 %collective-permute-start = (f32[4,128,256]{2,1,0:T(8,128)}, f32[4,128,256]{2,1,0:T(8,128)}, u32[]{:S(2)}, u32[]{:S(2)}) collective-permute-start(f32[4,128,256]{2,1,0:T(8,128)} %bitcast), channel_id=1, source_target_pairs={{0,1},{1,2},{2,3},{3,4},{4,5},{5,6},{6,7},{7,8},{8,9},{9,10},{10,1... | collective-permute-start | bytes 1572872 | tf_op jit(solution)/shard_map/ppermute | solution.py:19
  12.2 14.1 %copy-start.16 = (s32[96]{0:T(128)S(1)}, s32[96]{0:T(128)}, u32[]{:S(2)}) copy-start(s32[96]{0:T(128)} %param.23) | copy-start | bytes 1156
  38.9 2.3 copy-start.10
  41.2 5.4 copy-start.17
  42.3 80.6 %collective-permute-start.2 = (f32[4,128,256]{2,1,0:T(8,128)}, f32[4,128,256]{2,1,0:T(8,128)S(1)}, u32[]{:S(2)}, u32[]{:S(2)}) collective-permute-start(f32[4,128,256]{2,1,0:T(8,128)} %copy.132), channel_id=1, source_target_pairs={{0,1},{1,2},{2,3},{3,4},{4,5},{5,6},{6,7},{7,8},{8,9},{9,10},{10,1... | collective-permute-start | bytes 1572872 | tf_op jit(solution)/shard_map/ppermute | solution.py:19
  43.7 81.1 %collective-permute-start.3 = (f32[4,128,256]{2,1,0:T(8,128)}, f32[4,128,256]{2,1,0:T(8,128)}, u32[]{:S(2)}, u32[]{:S(2)}) collective-permute-start(f32[4,128,256]{2,1,0:T(8,128)} %copy.133), channel_id=1, source_target_pairs={{1,0},{2,1},{3,2},{4,3},{5,4},{6,5},{7,6},{8,7},{9,8},{10,9},{11,1... | collective-permute-start | bytes 1572872 | tf_op jit(solution)/shard_map/ppermute | solution.py:22
  47.3 27.4 %all-to-all-start = ((s32[4,1,2]{2,1,0:T(1,128)}), s32[4,1,2]{2,1,0:T(1,128)S(1)}, u32[]{:S(2)}, u32[]{:S(2)}) async-start(s32[4,1,2]{2,1,0:T(1,128)} %copy.87), calls=%async_computation | async-start | bytes 4096 | tf_op jit(solution)/shard_map/all_to_all | solution.py:52
  52.4 11.0 %copy-start.15 = (s32[4,2]{0,1:T(2,128)S(1)}, s32[4,2]{0,1:T(2,128)}, u32[]{:S(2)}) copy-start(s32[4,2]{0,1:T(2,128)} %param.25) | copy-start | bytes 100
  74.7 43.7 %all-to-all-start.2 = ((f32[4,2,128,256]{2,3,1,0:T(8,128)}), f32[4,2,128,256]{2,3,1,0:T(8,128)S(1)}, u32[]{:S(2)}, u32[]{:S(2)}) async-start(f32[4,2,128,256]{2,3,1,0:T(8,128)} %convolution_bitcast_fusion.3), calls=%async_computation.2 | async-start | bytes 2097152 | tf_op jit(solution)/shard_map/all_to_all | solution.py:61
  118.5 14.9 %all-to-all-start.1 = ((f32[4,2,128,256]{2,3,1,0:T(8,128)}), f32[4,2,128,256]{2,3,1,0:T(8,128)S(1)}, u32[]{:S(2)}, u32[]{:S(2)}) async-start(f32[4,2,128,256]{2,3,1,0:T(8,128)} %bitcast.15), calls=%async_computation.1 | async-start | bytes 2097152 | tf_op jit(solution)/shard_map/all_to_all | solution.py:60
  122.7 182.3 %all-reduce.10.cloned.1.call-start = ((), (), s32[]{:S(2)}) async-start(), calls=%async_computation.7 | async-start | bytes 1048576 | tf_op jit(solution)/shard_map/psum | solution.py:85
  134.9 2.2 copy-start.8
  137.1 7.2 copy-start.1
  137.1 7.2 copy-start.14
  145.6 2.0 copy-start.6
  155.4 370.8 %all-reduce.6.cloned.1.call-start = ((), (), s32[]{:S(2)}) async-start(), calls=%async_computation.5 | async-start | bytes 524288 | tf_op jit(solution)/shard_map/psum | solution.py:85
  305.0 61.9 %copy-start.12 = (f32[256,256]{0,1:T(8,128)S(1)}, f32[256,256]{0,1:T(8,128)}, u32[]{:S(2)}) copy-start(f32[256,256]{0,1:T(8,128)} %get-tuple-element.129) | copy-start | bytes 786436
  375.8 2.0 copy-start.5
  536.6 2.0 copy-start.2
  584.9 12.9 %collective-permute-start.5 = (f32[4,128,256]{2,1,0:T(8,128)}, f32[4,128,256]{2,1,0:T(8,128)}, u32[]{:S(2)}, u32[]{:S(2)}) collective-permute-start(f32[4,128,256]{2,1,0:T(8,128)} %bitcast.43), channel_id=1, source_target_pairs={{1,0},{2,1},{3,2},{4,3},{5,4},{6,5},{7,6},{8,7},{9,8},{10,9},{11,1... | collective-permute-start | bytes 1572872 | tf_op jit(solution)/shard_map/ppermute | solution.py:22
  586.0 11.8 %collective-permute-start.4 = (f32[4,128,256]{2,1,0:T(8,128)}, f32[4,128,256]{2,1,0:T(8,128)}, u32[]{:S(2)}, u32[]{:S(2)}) collective-permute-start(f32[4,128,256]{2,1,0:T(8,128)} %bitcast.41), channel_id=1, source_target_pairs={{0,1},{1,2},{2,3},{3,4},{4,5},{5,6},{6,7},{7,8},{8,9},{9,10},{10,1... | collective-permute-start | bytes 1572872 | tf_op jit(solution)/shard_map/ppermute | solution.py:19
  587.8 47.9 %collective-permute-start.6 = (f32[4,128,256]{2,1,0:T(8,128)}, f32[4,128,256]{2,1,0:T(8,128)S(1)}, u32[]{:S(2)}, u32[]{:S(2)}) collective-permute-start(f32[4,128,256]{2,1,0:T(8,128)} %copy.135), channel_id=1, source_target_pairs={{0,1},{1,2},{2,3},{3,4},{4,5},{5,6},{6,7},{7,8},{8,9},{9,10},{10,1... | collective-permute-start | bytes 1572872 | tf_op jit(solution)/shard_map/ppermute | solution.py:19
  588.6 49.0 %collective-permute-start.7 = (f32[4,128,256]{2,1,0:T(8,128)}, f32[4,128,256]{2,1,0:T(8,128)}, u32[]{:S(2)}, u32[]{:S(2)}) collective-permute-start(f32[4,128,256]{2,1,0:T(8,128)} %copy.136), channel_id=1, source_target_pairs={{1,0},{2,1},{3,2},{4,3},{5,4},{6,5},{7,6},{8,7},{9,8},{10,9},{11,1... | collective-permute-start | bytes 1572872 | tf_op jit(solution)/shard_map/ppermute | solution.py:22
  593.0 38.1 %all-to-all-start.4 = ((f32[4,2,128,256]{2,3,1,0:T(8,128)}), f32[4,2,128,256]{2,3,1,0:T(8,128)S(1)}, u32[]{:S(2)}, u32[]{:S(2)}) async-start(f32[4,2,128,256]{2,3,1,0:T(8,128)} %convolution_bitcast_fusion.2), calls=%async_computation.4 | async-start | bytes 2097152 | tf_op jit(solution)/shard_map/all_to_all | solution.py:61
  631.1 15.2 %all-to-all-start.3 = ((f32[4,2,128,256]{2,3,1,0:T(8,128)}), f32[4,2,128,256]{2,3,1,0:T(8,128)S(1)}, u32[]{:S(2)}, u32[]{:S(2)}) async-start(f32[4,2,128,256]{2,3,1,0:T(8,128)} %bitcast.51), calls=%async_computation.3 | async-start | bytes 2097152 | tf_op jit(solution)/shard_map/all_to_all | solution.py:60
  635.3 178.3 %all-reduce.8.cloned.1.call-start = ((), (), s32[]{:S(2)}) async-start(), calls=%async_computation.6 | async-start | bytes 524288 | tf_op jit(solution)/shard_map/psum | solution.py:85
  647.8 2.2 copy-start.9
  650.0 7.2 copy-start.3
  658.4 1.9 copy-start.7
  680.9 195.7 %copy-start.13 = (f32[256,256]{1,0:T(8,128)S(1)}, f32[256,256]{1,0:T(8,128)}, u32[]{:S(2)}) copy-start(f32[256,256]{1,0:T(8,128)} %all-reduce.6.cloned.1.call-done) | copy-start | bytes 786436
  878.3 9.1 %copy-start.4 = (f32[4096,256]{1,0:T(8,128)S(1)}, f32[4096,256]{1,0:T(8,128)}, u32[]{:S(2)}) copy-start(f32[4096,256]{1,0:T(8,128)} %copy-done.2) | copy-start | bytes 12582916
  878.3 9.1 %copy-start.11 = (f32[4096,256]{0,1:T(8,128)S(1)}, f32[4096,256]{0,1:T(8,128)}, u32[]{:S(2)}) copy-start(f32[4096,256]{0,1:T(8,128)} %convolution_bitcast_fusion.1) | copy-start | bytes 12582916
Sparse Core Ops, SparseCore 0:
  155.5 149.4 all-reduce.9
  385.4 140.7 all-reduce.5
  668.3 145.2 all-reduce.7
where the time goes:
time: 912 us; the launch traced here: 905 us
  waiting for transfers between devices  363 us (40%)
  other arithmetic  201 us (22%)
  matrix products  190 us (21%)
  local copies, waits for them, and re-layouts  101 us (11%)
  starting transfers between devices  32 us (4%)
  between operations  18.7 us (2%)
    psum x3, waiting for transfers between devices, summed(): return lax.psum(local, ('blk', 'grp'))  363 us
    another operation x19, other arithmetic, chol_solve(): factor = jnp.linalg.cholesky(matrix)  103 us
    another operation x7, other arithmetic, chol_solve(): lax.linalg.triangular_solve(factor, middle, left_side=True, lower=True, t...  59.9 us
    dot_general x6, matrix products, spread_rows(): return jnp.einsum('kq,kan->qan', selector, terms, precision=HIGH)  34.9 us
    dot_general x4, matrix products, inner(): return jnp.einsum('nc,nd->cd', left, right, precision=HIGH)  34 us
    dot_general x2, matrix products, operate(): forward = jnp.einsum('rjab,rjbn->ran', near_mats, partner, precision=HIGH)  33.5 us
    dot_general x2, matrix products, operate(): jnp.einsum('rjba,rbn->rjan', near_mats, slab_blocks, precision=HIGH)  30.1 us
    gather x2, local copies, waits for them, and re-layouts, operate(): partner = extended[near_cols].reshape(brows, NEAR_PER, block, cases)  22.3 us
  transfers between devices with their start and end apart: 16, of which 3 were waited for; matrix products, arithmetic and copies ran while one was open for 25% of the time, Pallas kernels for 0%

commit v1 on v0

v1 whole, which is shorter than its diff:
```python
import functools

import jax
import jax.numpy as jnp
from jax import lax
from jax.experimental import pallas as pl
from jax.experimental.pallas import tpu as pltpu
from jax.sharding import PartitionSpec as P

NEAR_PER = 3
HB = 4
SHORT = 2
N_BLK = 4
MESH = pl.DeviceIdType.MESH
HIGH = lax.Precision.HIGHEST
F32 = jnp.float32
BF16 = jnp.bfloat16
VMEM_LIMIT = 60 * 1024 * 1024

PERM, KEEP, LAST, SPERM, SKEEP, SLAST, PLAN = 0, 96, 192, 240, 248, 256, 320


def split(x):
    hi = x.astype(BF16)
    lo = (x - hi.astype(F32)).astype(BF16)
    return hi, lo


def dot(a, b):
    return jnp.dot(a, b, preferred_element_type=F32)


def dot_t(a, b):
    return lax.dot_general(a, b, (((0,), (0,)), ((), ())), preferred_element_type=F32)


def plan_kernel(cols_ref, rows_ref, scols_ref, plan_ref, tile_ref, count, start):
    def order(keys, n_keys, n_dest, perm_at, keep_at, last_at):
        def clear(q, c):
            count[q] = 0
            return c

        lax.fori_loop(0, n_dest, clear, 0)

        def tally(m, c):
            q = keys(m)
            count[q] = count[q] + 1
            return c

        lax.fori_loop(0, n_keys, tally, 0)

        def prefix(q, run):
            start[q] = run
            end = run + count[q]
            plan_ref[last_at + q] = jnp.where(count[q] > 0, end, 0)
            count[q] = run
            return end

        lax.fori_loop(0, n_dest, prefix, jnp.int32(0))

        def place(m, c):
            q = keys(m)
            p = start[q]
            start[q] = p + 1
            plan_ref[perm_at + p] = m
            plan_ref[keep_at + p] = jnp.where(p > count[q], 1, 0)
            return c

        lax.fori_loop(0, n_keys, place, 0)

    order(lambda m: cols_ref[m], 96, 40, PERM, KEEP, LAST)
    order(lambda m: rows_ref[m], 8, 32, SPERM, SKEEP, SLAST)
    row = lax.broadcasted_iota(jnp.int32, (8, 128), 0)
    lane = lax.broadcasted_iota(jnp.int32, (8, 128), 1)
    tile = jnp.zeros((8, 128), jnp.int32)
    for c in range(N_BLK):
        for s in range(SHORT):
            tile = jnp.where((row == c) & (lane == s), scols_ref[c * SHORT + s], tile)
    tile_ref[...] = tile


def make_plan(near_cols, short_rows, short_cols):
    smem = pl.BlockSpec(memory_space=pltpu.SMEM)
    return pl.pallas_call(
        plan_kernel,
        out_shape=(
            jax.ShapeDtypeStruct((PLAN,), jnp.int32),
            jax.ShapeDtypeStruct((8, 128), jnp.int32),
        ),
        in_specs=[smem, smem, smem],
        out_specs=(smem, pl.BlockSpec(memory_space=pltpu.VMEM)),
        scratch_shapes=[pltpu.SMEM((48,), jnp.int32), pltpu.SMEM((48,), jnp.int32)],
        name="plan",
    )(near_cols, short_rows.reshape(-1), short_cols.reshape(-1))


def apply_kernel(
    plan, scols, field, diag, near, short, tile,
    image, grams,
    fv, ext, wn, ws, seg, out, halo, rim_out, rim_in, trm_out, trm, fet_out, fet, rseg,
    idx_in, idx_sm, acc_h, acc_l, acc_y,
    load_sem, out_sem, idx_sem, halo_send, halo_recv, idx_send, idx_recv, trm_send, trm_recv,
    fet_send, fet_recv, rim_send, rim_recv,
):
    brows = field.shape[0]
    b = lax.axis_index("blk")
    g = lax.axis_index("grp")
    n_grp = lax.axis_size("grp")
    left = (b, lax.rem(g + n_grp - 1, n_grp))
    right = (b, lax.rem(g + 1, n_grp))
    peers = [None] + [(lax.rem(b + d, N_BLK), g) for d in range(1, N_BLK)]

    loads = [
        pltpu.make_async_copy(field, fv, load_sem.at[0]),
        pltpu.make_async_copy(short, ws, load_sem.at[1]),
        pltpu.make_async_copy(near, wn, load_sem.at[2]),
    ]
    for copy in loads:
        copy.start()

    barrier = pltpu.get_barrier_semaphore()
    for peer in [left, right] + peers[1:]:
        pl.semaphore_signal(barrier, inc=1, device_id=peer, device_id_type=MESH)
    pl.semaphore_wait(barrier, 5)

    def remote(src, dst, send, recv, peer):
        copy = pltpu.make_async_remote_copy(
            src_ref=src, dst_ref=dst, send_sem=send, recv_sem=recv,
            device_id=peer, device_id_type=MESH,
        )
        copy.start()
        return copy

    idx_copies = [
        remote(tile, idx_in.at[3 - d], idx_send.at[d - 1], idx_recv.at[3 - d], peers[d])
        for d in range(1, N_BLK)
    ]
    halo_copies = [
        remote(field.at[pl.ds(0, HB)], halo.at[pl.ds(HB, HB)], halo_send.at[0], halo_recv.at[0], left),
        remote(field.at[pl.ds(brows - HB, HB)], halo.at[pl.ds(0, HB)], halo_send.at[1], halo_recv.at[1], right),
    ]

    loads[0].wait()
    loads[1].wait()

    def split_own(r, c):
        hi, lo = split(fv[r])
        ext[HB + r, :128, :] = hi
        ext[HB + r, 128:, :] = lo
        return c

    lax.fori_loop(0, brows, split_own, 0)

    def three(w, e):
        hi, lo = split(w)
        return dot(jnp.concatenate([hi, hi, lo], axis=1), jnp.concatenate([e, e[:128]], axis=0))

    for d in range(N_BLK):
        c = lax.rem(b + d, N_BLK)
        for s in range(SHORT):
            n = c * SHORT + s
            e = ext[HB + plan_rows(scols, n)]
            term = three(ws[n].T, e)
            if d == 0:
                trm[s] = term
            else:
                trm_out[(d - 1) * SHORT + s] = term
    trm_copies = []
    for d in (1, 3, 2):
        trm_copies.append(
            remote(
                trm_out.at[pl.ds((d - 1) * SHORT, SHORT)], trm.at[pl.ds((4 - d) * SHORT, SHORT)],
                trm_send.at[d - 1], trm_recv.at[3 - d], peers[d],
            )
        )

    for copy in idx_copies:
        copy.wait()
    local = pltpu.make_async_copy(idx_in, idx_sm, idx_sem)
    local.start()
    local.wait()
    for d in range(N_BLK):
        for s in range(SHORT):
            if d == 0:
                fet[s] = fv[scols[8 + b * SHORT + s]]
            else:
                fet_out[(d - 1) * SHORT + s] = fv[idx_sm[d - 1, b, s]]
    fet_copies = []
    for d in (1, 3, 2):
        fet_copies.append(
            remote(
                fet_out.at[pl.ds((d - 1) * SHORT, SHORT)], fet.at[pl.ds((4 - d) * SHORT, SHORT)],
                fet_send.at[d - 1], fet_recv.at[3 - d], peers[d],
            )
        )

    loads[2].wait()
    seg[0] = jnp.zeros(seg.shape[1:], F32)

    def backward(i, carry):
        for u in range(2):
            k = i * 2 + u
            m = plan[PERM + k]
            keep = plan[KEEP + k].astype(F32)
            term = three(wn[m].T, ext[HB + lax.div(m, NEAR_PER)])
            seg[k + 1] = seg[k] * keep + term
        return carry

    lax.fori_loop(0, brows * NEAR_PER // 2, backward, 0)
    for q in range(HB):
        rim_out[q] = seg[plan[LAST + q]]
        rim_out[HB + q] = seg[plan[LAST + HB + brows + q]]
    rim_copies = [
        remote(rim_out.at[pl.ds(0, HB)], rim_in.at[pl.ds(HB, HB)], rim_send.at[0], rim_recv.at[0], left),
        remote(rim_out.at[pl.ds(HB, HB)], rim_in.at[pl.ds(0, HB)], rim_send.at[1], rim_recv.at[1], right),
    ]

    acc_h[...] = jnp.zeros(acc_h.shape, F32)
    acc_l[...] = jnp.zeros(acc_l.shape, F32)
    acc_y[...] = jnp.zeros(acc_y.shape, F32)
    per = 4

    def gram(i, c):
        hi = ext[pl.ds(HB + i * per, per), :128, :].reshape(per * 128, 256)
        lo = ext[pl.ds(HB + i * per, per), 128:, :].reshape(per * 128, 256)
        acc_h[...] += dot_t(hi, hi)
        acc_l[...] += dot_t(hi, lo)
        acc_h[...] += dot_t(lo, lo)
        return c

    lax.fori_loop(0, brows // per, gram, 0)

    for copy in halo_copies:
        copy.wait()

    def split_halo(q, c):
        hi, lo = split(halo[q])
        at = jnp.where(q < HB, q, q + brows)
        ext[at, :128, :] = hi
        ext[at, 128:, :] = lo
        return c

    lax.fori_loop(0, 2 * HB, split_halo, 0)

    def half_diag(r):
        d = jnp.broadcast_to(diag[pl.ds(r, 1), :], (128, 128)).T * 0.5
        return jnp.concatenate([d, d], axis=1) * fv[r]

    def forward(r, c):
        lhs, rhs = [], []
        for j in range(NEAR_PER):
            m = r * NEAR_PER + j
            hi, lo = split(wn[m])
            e = ext[scols[16 + m]]
            lhs += [hi, hi, lo]
            rhs += [e, e[:128]]
        out[r] = half_diag(r) + dot(jnp.concatenate(lhs, axis=1), jnp.concatenate(rhs, axis=0))
        return c

    lax.fori_loop(0, brows, forward, 0)

    for copy in fet_copies:
        copy.wait()
    rseg[0] = jnp.zeros(rseg.shape[1:], F32)
    for i in range(N_BLK * SHORT):
        n = plan[SPERM + i]
        slot = lax.rem(lax.div(n, SHORT) + N_BLK - b, N_BLK) * SHORT + lax.rem(n, SHORT)
        hi, lo = split(fet[slot])
        term = three(ws[n], jnp.concatenate([hi, lo], axis=0))
        rseg[i + 1] = rseg[i] * plan[SKEEP + i].astype(F32) + term

    def gram_y(i, c):
        parts = []
        for u in range(per):
            r = i * per + u
            f = out[r] + rseg[plan[SLAST + r]]
            out[r] = f
            parts.append(f)
        fh, fl = split(jnp.concatenate(parts, axis=0))
        hi = ext[pl.ds(HB + i * per, per), :128, :].reshape(per * 128, 256)
        lo = ext[pl.ds(HB + i * per, per), 128:, :].reshape(per * 128, 256)
        acc_y[...] += dot_t(hi, fh) + dot_t(hi, fl) + dot_t(lo, fh)
        return c

    lax.fori_loop(0, brows // per, gram_y, 0)
    low = acc_l[...]
    grams[0] = acc_h[...] + (low + low.T)
    y = acc_y[...]
    grams[1] = y + y.T

    for copy in trm_copies:
        copy.wait()
    dest = [scols[8 + b * SHORT + s] for s in range(SHORT)]
    for d in range(1, N_BLK):
        dest += [idx_sm[d - 1, b, s] for s in range(SHORT)]

    def finish(r, c):
        total = out[r] + half_diag(r) + seg[plan[LAST + HB + r]]
        for i in range(N_BLK * SHORT):
            total += trm[i] * jnp.where(dest[i] == r, 1.0, 0.0)
        out[r] = total
        return c

    lax.fori_loop(0, brows, finish, 0)
    for copy in rim_copies:
        copy.wait()
    for q in range(HB):
        out[q] = out[q] + rim_in[q]
        out[brows - HB + q] = out[brows - HB + q] + rim_in[HB + q]
    copy = pltpu.make_async_copy(out, image, out_sem)
    copy.start()
    copy.wait()


def plan_rows(scols, n):
    return scols[n]


def apply(plan, scols, field, diag, near, short, tile):
    brows = field.shape[0]
    smem = pl.BlockSpec(memory_space=pltpu.SMEM)
    vmem = pl.BlockSpec(memory_space=pltpu.VMEM)
    hbm = pl.BlockSpec(memory_space=pl.ANY)
    block = lambda n: pltpu.VMEM((n, 128, 256), F32)
    dma = pltpu.SemaphoreType.DMA
    return pl.pallas_call(
        apply_kernel,
        out_shape=(
            jax.ShapeDtypeStruct(field.shape, F32),
            jax.ShapeDtypeStruct((2, 256, 256), F32),
        ),
        in_specs=[smem, smem, hbm, vmem, hbm, hbm, vmem],
        out_specs=(hbm, vmem),
        scratch_shapes=[
            block(brows),
            pltpu.VMEM((brows + 2 * HB, 256, 256), BF16),
            pltpu.VMEM(near.shape, F32),
            pltpu.VMEM(short.shape, F32),
            block(brows * NEAR_PER + 1),
            block(brows),
            block(2 * HB), block(2 * HB), block(2 * HB),
            block(6), block(8), block(6), block(8), block(9),
            pltpu.VMEM((3, 8, 128), jnp.int32),
            pltpu.SMEM((3, 8, 128), jnp.int32),
            pltpu.VMEM((256, 256), F32), pltpu.VMEM((256, 256), F32), pltpu.VMEM((256, 256), F32),
            dma((3,)), dma, dma,
            dma((2,)), dma((2,)), dma((3,)), dma((3,)), dma((3,)), dma((3,)), dma((3,)), dma((3,)),
            dma((2,)), dma((2,)),
        ],
        compiler_params=pltpu.CompilerParams(
            collective_id=0, has_side_effects=True, vmem_limit_bytes=VMEM_LIMIT
        ),
        name="apply",
    )(plan, scols, field, diag, near, short, tile)


def reduce_kernel(x, res, buf_a, part, buf_b, mid, sa, ra, sb, rb, sc, rc, sd, rd):
    b = lax.axis_index("blk")
    g = lax.axis_index("grp")
    n_grp = lax.axis_size("grp")
    core = lax.rem(g, 2)
    plane = lax.div(g, 2)
    n_a, n_b = N_BLK * 2, n_grp // 2
    a = b * 2 + core
    rows_a = x.shape[0] // n_a
    rows_b = rows_a // n_b
    a_peers = []
    for i in range(1, n_a):
        t = lax.rem(a + i, n_a)
        a_peers.append((t, (lax.div(t, 2), plane * 2 + lax.rem(t, 2))))
    b_peers = []
    for i in range(1, n_b):
        t = lax.rem(plane + i, n_b)
        b_peers.append((t, (b, t * 2 + core)))

    barrier = pltpu.get_barrier_semaphore()
    for _, peer in a_peers + b_peers:
        pl.semaphore_signal(barrier, inc=1, device_id=peer, device_id_type=MESH)
    pl.semaphore_wait(barrier, len(a_peers) + len(b_peers))

    def remote(src, dst, send, recv, peer):
        copy = pltpu.make_async_remote_copy(
            src_ref=src, dst_ref=dst, send_sem=send, recv_sem=recv,
            device_id=peer, device_id_type=MESH,
        )
        copy.start()
        return copy

    def piece(ref, at, rows):
        return ref.at[pl.ds(pl.multiple_of(at * rows, rows), rows)]

    copies = []
    for i, (t, peer) in enumerate(a_peers):
        copies.append(remote(piece(x, t, rows_a), buf_a.at[n_a - 2 - i], sa.at[i], ra.at[n_a - 2 - i], peer))
    total = x[pl.ds(pl.multiple_of(a * rows_a, rows_a), rows_a)]
    for copy in copies:
        copy.wait()
    for i in range(n_a - 1):
        total += buf_a[i]
    part[...] = total

    copies = []
    for i, (t, peer) in enumerate(b_peers):
        copies.append(remote(piece(part, t, rows_b), buf_b.at[n_b - 2 - i], sb.at[i], rb.at[n_b - 2 - i], peer))
    total = part[pl.ds(pl.multiple_of(plane * rows_b, rows_b), rows_b)]
    for copy in copies:
        copy.wait()
    for i in range(n_b - 1):
        total += buf_b[i]
    mid[pl.ds(pl.multiple_of(plane * rows_b, rows_b), rows_b)] = total

    copies = []
    for i, (t, peer) in enumerate(b_peers):
        copies.append(remote(piece(mid, plane, rows_b), piece(mid, plane, rows_b), sc.at[i], rc.at[n_b - 2 - i], peer))
    for copy in copies:
        copy.wait()

    res[pl.ds(pl.multiple_of(a * rows_a, rows_a), rows_a)] = mid[...]
    copies = []
    for i, (t, peer) in enumerate(a_peers):
        copies.append(remote(mid, piece(res, a, rows_a), sd.at[i], rd.at[n_a - 2 - i], peer))
    for copy in copies:
        copy.wait()


def reduce_all(x):
    n_a, n_b = 8, 16
    rows_a = x.shape[0] // n_a
    rows_b = rows_a // n_b
    vmem = pl.BlockSpec(memory_space=pltpu.VMEM)
    dma = pltpu.SemaphoreType.DMA
    return pl.pallas_call(
        reduce_kernel,
        out_shape=jax.ShapeDtypeStruct(x.shape, F32),
        in_specs=[vmem],
        out_specs=vmem,
        scratch_shapes=[
            pltpu.VMEM((n_a - 1, rows_a, 256), F32),
            pltpu.VMEM((rows_a, 256), F32),
            pltpu.VMEM((n_b - 1, rows_b, 256), F32),
            pltpu.VMEM((rows_a, 256), F32),
            dma((n_a - 1,)), dma((n_a - 1,)), dma((n_b - 1,)), dma((n_b - 1,)),
            dma((n_b - 1,)), dma((n_b - 1,)), dma((n_a - 1,)), dma((n_a - 1,)),
        ],
        compiler_params=pltpu.CompilerParams(
            collective_id=1, has_side_effects=True, vmem_limit_bytes=VMEM_LIMIT
        ),
        name="reduce",
    )(x)


def mm(a, b):
    return jnp.dot(a, b, precision=HIGH, preferred_element_type=F32)


def sweep_inverse(mats):
    n = mats[0].shape[0]
    row_at = lax.broadcasted_iota(jnp.int32, (n, n), 0)
    col_at = lax.broadcasted_iota(jnp.int32, (n, n), 1)
    mats = list(mats)
    for k in range(n):
        for i, m in enumerate(mats):
            row = m[k : k + 1, :]
            col = m[:, k : k + 1]
            inv = 1.0 / m[k : k + 1, k : k + 1]
            scaled = row * inv
            new = m - col * scaled
            new = jnp.where(row_at == k, scaled, new)
            new = jnp.where(col_at == k, jnp.where(row_at == k, -inv, col * inv), new)
            mats[i] = new
    return [-m for m in mats]


def spd_inverse(mats):
    h = mats[0].shape[0] // 2
    top = sweep_inverse([m[:h, :h] for m in mats])
    left = [mm(m[h:, :h], t) for m, t in zip(mats, top)]
    schur = sweep_inverse([m[h:, h:] - mm(l, m[:h, h:]) for m, l in zip(mats, left)])
    result = []
    for t, l, s in zip(top, left, schur):
        sl = mm(s, l)
        upper = jnp.concatenate([t + mm(l.T, sl), -sl.T], axis=1)
        lower = jnp.concatenate([-sl, s], axis=1)
        result.append(jnp.concatenate([upper, lower], axis=0))
    return result


def solve(matrix, inverse, rhs):
    x = mm(inverse, rhs)
    return x + mm(inverse, rhs - mm(matrix, x))


def algebra_kernel(grams, cd):
    rr0, g01, g11, g12 = (grams[i * 256 : (i + 1) * 256, :] for i in range(4))
    inv0, inv1 = spd_inverse([rr0, g01])
    a1 = solve(g01, inv1, rr0)
    ga = mm(g01, a1)
    g11a = mm(g11, a1)
    rr1 = rr0 - ga - ga.T + mm(a1.T, g11a)
    rr1 = 0.5 * (rr1 + rr1.T)
    b1 = solve(rr0, inv0, rr1)
    eye = jnp.where(
        lax.broadcasted_iota(jnp.int32, (256, 256), 0) == lax.broadcasted_iota(jnp.int32, (256, 256), 1), 1.0, 0.0
    )
    t = eye + b1
    cross = mm(t.T, g11a)
    pq2 = mm(t.T, mm(g01, t)) - cross - cross.T + mm(a1.T, mm(g12, a1))
    pq2 = 0.5 * (pq2 + pq2.T)
    (inv2,) = spd_inverse([pq2])
    a2 = solve(pq2, inv2, rr1)
    c = a1 + mm(t, a2)
    d = mm(a1, a2)
    cd[0], cd[1] = split(c)
    cd[2], cd[3] = split(d)


def algebra(grams):
    vmem = pl.BlockSpec(memory_space=pltpu.VMEM)
    return pl.pallas_call(
        algebra_kernel,
        out_shape=jax.ShapeDtypeStruct((4, 256, 256), BF16),
        in_specs=[vmem],
        out_specs=vmem,
        compiler_params=pltpu.CompilerParams(vmem_limit_bytes=VMEM_LIMIT),
        name="algebra",
    )(grams)


def final_kernel(cd, r0, q1, s, sol, res):
    c_hi, c_lo, d_hi, d_lo = cd[0], cd[1], cd[2], cd[3]
    r_hi, r_lo = split(r0[...])
    q_hi, q_lo = split(q1[...])
    s_hi, s_lo = split(s[...])

    def three(hi, lo, w_hi, w_lo):
        return dot(hi, w_hi) + (dot(hi, w_lo) + dot(lo, w_hi))

    sol[...] = three(r_hi, r_lo, c_hi, c_lo) - three(q_hi, q_lo, d_hi, d_lo)
    res[...] = r0[...] - three(q_hi, q_lo, c_hi, c_lo) + three(s_hi, s_lo, d_hi, d_lo)


def final(cd, r0, q1, s):
    rows = r0.shape[0]
    tile = 512
    spec = pl.BlockSpec((tile, 256), lambda i: (i, 0))
    return pl.pallas_call(
        final_kernel,
        grid=(rows // tile,),
        out_shape=(jax.ShapeDtypeStruct(r0.shape, F32),) * 2,
        in_specs=[pl.BlockSpec((4, 256, 256), lambda i: (0, 0, 0)), spec, spec, spec],
        out_specs=(spec, spec),
        compiler_params=pltpu.CompilerParams(vmem_limit_bytes=VMEM_LIMIT),
        name="final",
    )(cd, r0, q1, s)


def body(loads, pore_diag, near_blocks, near_cols, short_blocks, short_rows, short_cols):
    rows, cases = loads.shape
    brows = rows // 128
    plan, tile = make_plan(near_cols, short_rows, short_cols)
    scols = jnp.concatenate([short_rows.reshape(-1), short_cols.reshape(-1), near_cols])
    diag = pore_diag.reshape(brows, 128)
    short = short_blocks.reshape(-1, 128, 128)
    field = loads.reshape(brows, 128, cases)
    q1, g1 = apply(plan, scols, field, diag, near_blocks, short, tile)
    s, g2 = apply(plan, scols, q1, diag, near_blocks, short, tile)
    grams = reduce_all(jnp.concatenate([g1, g2], axis=0).reshape(4 * 256, 256))
    cd = algebra(grams)
    return final(cd, loads, q1.reshape(rows, cases), s.reshape(rows, cases))


def solution(mesh):
    in_specs = (
        P(("blk", "grp"), None),
        P(("blk", "grp")),
        P(("blk", "grp"), None, None),
        P(("blk", "grp")),
        P(("blk", "grp"), None, None, None),
        P(("blk", "grp"), None),
        P(("blk", "grp"), None),
    )
    out_specs = (P(("blk", "grp"), None), P(("blk", "grp"), None))
    return jax.shard_map(body, mesh=mesh, in_specs=in_specs, out_specs=out_specs, check_vma=False)
```

time: 912 us -> 249 us (0.27)
  waiting for transfers between devices: 363 us -> 0 us
  Pallas kernels: 0 us -> 238 us
  other arithmetic: 201 us -> 3.35 us
  matrix products: 190 us -> 0 us
  local copies, waits for them, and re-layouts: 101 us -> 1.71 us
  starting transfers between devices: 32 us -> 0 us
  between operations: 18.7 us -> 0.87 us
    psum x3 -> x0, waiting for transfers between devices: 363 us -> none  [summed(): return lax.psum(local, ('blk', 'grp'))]
    pallas_call x0 -> x6, Pallas kernels: none -> 238 us  [the longest x2 91.6 us: apply(): pl.pallas_call(apply_kernel, out_shape=(jax.ShapeDtypeStruct(field.shape,...]
    dot_general x23 -> x0, matrix products: 182 us -> none  [the longest x6 34.9 us: spread_rows(): return jnp.einsum('kq,kan->qan', selector, terms, precision=HIGH)]
    another operation x26 -> x0, other arithmetic: 163 us -> none  [the longest x19 103 us: chol_solve(): factor = jnp.linalg.cholesky(matrix)]
    gather x8 -> x0, local copies, waits for them, and re-layouts: 36.2 us -> none  [the longest x2 22.3 us: operate(): partner = extended[near_cols].reshape(brows, NEAR_PER, block, cases)]
    all_to_all x5 -> x0, starting transfers between devices: 21.6 us -> none  [the longest x2 8.44 us: shortcut(): lax.all_to_all(fetch, 'blk', split_axis=0, concat_axis=0, tiled=True)]
    unnamed x42 -> x8, local copies, waits for them, and re-layouts: 19.9 us -> 1.54 us
    add x4 -> x0, other arithmetic: 16.7 us -> none  [the longest x2 14.3 us: operate(): own = own + shortcut(slab_blocks)]
  transfers between devices with their start and end apart: 16 -> 0, of which waited for: 3 -> 0; matrix products, arithmetic and copies ran while one was open for 25% -> 0% of each run, Pallas kernels for 0% -> 0%
where the time goes in v1:
time: 249 us; the launch traced here: 244 us
  Pallas kernels  238 us (96%)
  other arithmetic  3.35 us (1%)
    pallas_call x2, Pallas kernels, apply(): pl.pallas_call(apply_kernel, out_shape=(jax.ShapeDtypeStruct(field.shape,...  91.6 us
    pallas_call x1, Pallas kernels, algebra(): pl.pallas_call(algebra_kernel, out_shape=jax.ShapeDtypeStruct((4, 256, 25...  85.2 us
    pallas_call x1, Pallas kernels, reduce_all(): pl.pallas_call(reduce_kernel, out_shape=jax.ShapeDtypeStruct(x.shape, F32...  44.2 us
    pallas_call x1, Pallas kernels, final(): pl.pallas_call(final_kernel, grid=(rows // tile,), out_shape=(jax.ShapeDt...  12.7 us

profile of v1, /device:TPU:1, one launch (start us, length us, event | category | flops | bytes accessed | tf_op | source)
XLA Modules:
  0.0 244.2 jit_solution(6177773324963635054)
XLA Ops:
  0.6 0.8 copy.11
  1.4 0.1 reshape.30.rows_ref
  1.5 0.0 copy-start.1
  1.5 0.8 copy.12
  2.3 0.1 reshape.31.scols_ref
  2.3 0.0 copy-start.2
  2.3 1.2 pad_add_fusion.scols
  3.6 0.0 copy-done.1
  3.6 0.0 copy-done.2
  3.6 4.5 %plan.1 = (s32[320]{0:T(512)}, s32[8,128]{1,0:T(8,128)}) custom-call(s32[96]{0:T(128)} %cols_ref.1, s32[8]{0:T(128)} %copy-done.1, s32[8]{0:T(128)} %copy-done.2), custom_call_target="tpu_custom_call" | custom-call | tf_op jit(solution)/shard_map/plan/pallas_call | solution.py:84
  8.1 46.0 %apply.2 = (f32[32,128,256]{2,1,0:T(8,128)}, f32[2,256,256]{2,1,0:T(8,128)}) custom-call(s32[320]{0:T(512)} %get-tuple-element.8.plan, s32[112]{0:T(128)} %pad_add_fusion.scols, f32[32,128,256]{2,1,0:T(8,128)} %bitcast.6, f32[32,128]{1,0:T(8,128)} %bitcast.12, f32[96,128,128]{2,1,0:T(8,128)} %near.3, f32[8,128,128]{2,1,0:T(8,128)} %bitcast.10, ...), custom_call_target="tpu_custom_call" | custom-call | tf_op jit(solution)/shard_map/apply/pallas_call | solution.py:326
  54.1 0.0 copy-start
  54.1 45.6 %apply.3 = (f32[32,128,256]{2,1,0:T(8,128)}, f32[2,256,256]{2,1,0:T(8,128)}) custom-call(s32[320]{0:T(512)} %get-tuple-element.8.plan, s32[112]{0:T(128)} %pad_add_fusion.scols, f32[32,128,256]{2,1,0:T(8,128)} %get-tuple-element.11.field, f32[32,128]{1,0:T(8,128)} %bitcast.13, f32[96,128,128]{2,1,0:T(8,128)} %near.3, f32[8,128,128]{2,1,0:T(8,128)} %bitcast.11, ...), custom_call_target="tpu_custom_call" | custom-call | tf_op jit(solution)/shard_map/apply/pallas_call | solution.py:326
  99.7 0.0 copy-done
  99.8 2.1 pad_maximum_fusion
  101.9 44.2 %reduce.1.grams = f32[1024,256]{1,0:T(8,128)} custom-call(f32[1024,256]{1,0:T(8,128)} %bitcast.9), custom_call_target="tpu_custom_call" | custom-call | tf_op jit(solution)/shard_map/reduce/pallas_call | solution.py:432
  146.1 85.2 %algebra.1.cd = bf16[4,256,256]{2,1,0:T(8,128)(2,1)} custom-call(f32[1024,256]{1,0:T(8,128)} %reduce.1.grams), custom_call_target="tpu_custom_call" | custom-call | tf_op jit(solution)/shard_map/algebra/pallas_call | solution.py:519
  231.3 12.7 %final.1 = (f32[4096,256]{1,0:T(8,128)}, f32[4096,256]{1,0:T(8,128)}) custom-call(bf16[4,256,256]{2,1,0:T(8,128)(2,1)} %algebra.1.cd, f32[4096,256]{1,0:T(8,128)} %r0.1, f32[4096,256]{1,0:T(8,128)} %bitcast.7, f32[4096,256]{1,0:T(8,128)} %bitcast.8), custom_call_target="tpu_custom_call" | custom-call | tf_op jit(solution)/shard_map/final/pallas_call | solution.py:546
Async XLA Ops:
  1.5 2.1 copy-start.1
  2.3 1.3 copy-start.2
  54.1 45.6 %copy-start = (f32[2,256,256]{2,1,0:T(8,128)S(1)}, f32[2,256,256]{2,1,0:T(8,128)}, u32[]{:S(2)}) copy-start(f32[2,256,256]{2,1,0:T(8,128)} %get-tuple-element.10) | copy-start | bytes 1572868

commit v2 on v0

v2 whole, which is shorter than its diff:
```python
import jax
import jax.numpy as jnp
from jax import lax
from jax.experimental import pallas as pl
from jax.experimental.pallas import tpu as pltpu
from jax.sharding import PartitionSpec as P

NEAR_PER = 3
HB = 4
SHORT = 2
N_BLK = 4
MESH = pl.DeviceIdType.MESH
HIGHEST = lax.Precision.HIGHEST
F32 = jnp.float32
BF16 = jnp.bfloat16
VMEM_LIMIT = 60 * 1024 * 1024

PERM, KEEP, LAST, SPERM, SKEEP, SLAST = range(6)


def split(x):
    hi = x.astype(BF16)
    lo = (x - hi.astype(F32)).astype(BF16)
    return hi, lo


def dot(a, b):
    return jnp.dot(a, b, preferred_element_type=F32)


def dot_t(a, b):
    return lax.dot_general(a, b, (((0,), (0,)), ((), ())), preferred_element_type=F32)


def three(w, e):
    hi, lo = split(w)
    return dot(jnp.concatenate([hi, hi, lo], axis=1), jnp.concatenate([e, e[:128]], axis=0))


def order(keys, n):
    square = (128, 128)
    at_col = lax.broadcasted_iota(jnp.int32, square, 0)
    at_row = lax.broadcasted_iota(jnp.int32, square, 1)
    lane = lax.broadcasted_iota(jnp.int32, (1, 128), 1)
    key = jnp.where(lane < n, keys, 64)
    both = key * 128 + lane
    key_col = jnp.broadcast_to(key, square).T
    both_col = jnp.broadcast_to(both, square).T

    def count(cond):
        return jnp.sum(jnp.where(cond, 1, 0), axis=0, keepdims=True)

    rank = count(both_col < jnp.broadcast_to(both, square))
    hit = jnp.broadcast_to(rank, square).T == at_row
    perm = jnp.sum(jnp.where(hit, at_col, 0), axis=0, keepdims=True)
    placed = jnp.sum(jnp.where(hit, key_col, 0), axis=0, keepdims=True)
    keep = jnp.where(count(key_col < jnp.broadcast_to(placed, square)) < lane, 1, 0)
    begin, end = count(key_col < at_row), count(key_col <= at_row)
    return perm, keep, jnp.where(end > begin, end, 0)


def lanes(values):
    lane = lax.broadcasted_iota(jnp.int32, (1, 128), 1)
    row = jnp.zeros((1, 128), jnp.int32)
    for i, value in enumerate(values):
        row = jnp.where(lane == i, value, row)
    return row


def krylov_kernel(
    cols, srows, scols, cols_row, field, diag, near, short,
    image, image2, grams1, grams2,
    f0, f1, ext, wn, ws, dsp, seg, rseg, tseg, halo, rim_out, rim_in, trm_out, trm_0, trm_1, fet_out, fet_0, fet_1,
    tile, idx_in, idx_sm, keyrow, plan_v, plan, tplan_v, tplan, acc_h, acc_l, acc_y,
    x1, buf1, part1, zbuf1, mid1, x2, buf2, part2, zbuf2, mid2,
    load_sem, out_sem, idx_sem, idx_send, idx_recv, halo_send, halo_recv, trm_send, trm_recv,
    fet_send, fet_recv, rim_send, rim_recv, red1_sem, zred1_sem, red2_sem, zred2_sem,
):
    brows = f0.shape[0]
    b = lax.axis_index("blk")
    g = lax.axis_index("grp")
    n_grp = lax.axis_size("grp")
    left = (b, lax.rem(g + n_grp - 1, n_grp))
    right = (b, lax.rem(g + 1, n_grp))
    peers = [None] + [(lax.rem(b + d, N_BLK), g) for d in range(1, N_BLK)]

    loads = [
        pltpu.make_async_copy(field, f0, load_sem.at[0]),
        pltpu.make_async_copy(short, ws, load_sem.at[1]),
        pltpu.make_async_copy(near, wn, load_sem.at[2]),
    ]
    for copy in loads:
        copy.start()

    barrier = pltpu.get_barrier_semaphore()

    def greet(i, c):
        peer = (b, lax.rem(g + i, n_grp))
        pl.semaphore_signal(barrier, inc=1, device_id=peer, device_id_type=MESH)
        return c

    lax.fori_loop(1, n_grp, greet, 0)
    for peer in peers[1:]:
        pl.semaphore_signal(barrier, inc=1, device_id=peer, device_id_type=MESH)

    def remote(src, dst, send, recv, peer):
        copy = pltpu.make_async_remote_copy(
            src_ref=src, dst_ref=dst, send_sem=send, recv_sem=recv,
            device_id=peer, device_id_type=MESH,
        )
        copy.start()
        return copy

    sub = lax.broadcasted_iota(jnp.int32, (8, 128), 0)
    lane = lax.broadcasted_iota(jnp.int32, (8, 128), 1)
    own = jnp.zeros((8, 128), jnp.int32)
    for c in range(N_BLK):
        for s in range(SHORT):
            own = jnp.where((sub == c) & (lane == s), scols[c, s], own)
    tile[...] = own
    pl.semaphore_wait(barrier, n_grp - 1 + N_BLK - 1)
    idx_copies = [
        remote(tile, idx_in.at[3 - d], idx_send.at[d - 1], idx_recv.at[3 - d], peers[d])
        for d in range(1, N_BLK)
    ]
    keyrow[...] = jnp.zeros(keyrow.shape, jnp.int32)
    keyrow[0:1, :96] = cols_row[...]
    plan_v[...] = jnp.zeros(plan_v.shape, jnp.int32)
    plan_v[0:1, :], plan_v[1:2, :], plan_v[2:3, :] = order(keyrow[0:1, :], 96)
    plan_v[3:4, :], plan_v[4:5, :], plan_v[5:6, :] = order(
        lanes([srows[c, s] for c in range(N_BLK) for s in range(SHORT)]), 8
    )
    plan_copy = pltpu.make_async_copy(plan_v, plan, idx_sem.at[0])
    plan_copy.start()

    def spread_diag(r, c):
        dsp[r] = jnp.broadcast_to(diag[pl.ds(r, 1), :], (128, 128)).T * 0.5
        return c

    lax.fori_loop(0, brows, spread_diag, 0)
    seg[0] = jnp.zeros(seg.shape[1:], F32)
    rseg[0] = jnp.zeros(rseg.shape[1:], F32)
    tseg[0] = jnp.zeros(tseg.shape[1:], F32)
    for copy in idx_copies:
        copy.wait()
    idx_copy = pltpu.make_async_copy(idx_in, idx_sm, idx_sem.at[1])
    idx_copy.start()
    idx_copy.wait()
    tplan_v[...] = jnp.zeros(tplan_v.shape, jnp.int32)
    wanted = [scols[b, s] for s in range(SHORT)]
    for d in range(1, N_BLK):
        wanted += [idx_sm[d - 1, b, s] for s in range(SHORT)]
    tplan_v[0:1, :], tplan_v[1:2, :], tplan_v[2:3, :] = order(lanes(wanted), 8)
    tplan_copy = pltpu.make_async_copy(tplan_v, tplan, idx_sem.at[2])
    tplan_copy.start()
    plan_copy.wait()
    tplan_copy.wait()

    class Reduce:
        def __init__(self, x, buf, part, zbuf, mid, res, sems, zsems):
            self.x, self.buf, self.part, self.zbuf, self.mid, self.res = x, buf, part, zbuf, mid, res
            self.sems, self.zsems = sems, zsems
            self.rows = x.shape[0] // n_grp

        def piece(self, ref, at):
            return ref.at[pl.ds(pl.multiple_of(at * self.rows, self.rows), self.rows)]

        def each(self, act):
            def step(i, c):
                act(i)
                return c

            lax.fori_loop(1, n_grp, step, 0)

        def spread(self, i):
            t = lax.rem(g + i, n_grp)
            return pltpu.make_async_remote_copy(
                src_ref=self.piece(self.x, t), dst_ref=self.buf.at[n_grp - 1 - i],
                send_sem=self.sems.at[0, i - 1], recv_sem=self.sems.at[1, n_grp - 1 - i],
                device_id=(b, t), device_id_type=MESH,
            )

        def share(self, i):
            t = lax.rem(g + i, n_grp)
            return pltpu.make_async_remote_copy(
                src_ref=self.mid, dst_ref=self.piece(self.res, g),
                send_sem=self.sems.at[2, i - 1], recv_sem=self.sems.at[3, n_grp - 1 - i],
                device_id=(b, t), device_id_type=MESH,
            )

        def scatter(self):
            self.each(lambda i: self.spread(i).start())

        def across(self):
            self.each(lambda i: self.spread(i).wait())
            total = self.x[pl.ds(pl.multiple_of(g * self.rows, self.rows), self.rows)]
            for i in range(n_grp - 1):
                total += self.buf[i]
            self.part[...] = total
            self.copies = [
                remote(self.part, self.zbuf.at[3 - d], self.zsems.at[0, d - 1], self.zsems.at[1, 3 - d], peers[d])
                for d in range(1, N_BLK)
            ]

        def gather(self):
            for copy in self.copies:
                copy.wait()
            total = jnp.zeros(self.part.shape, F32)
            for z in range(N_BLK):
                term = jnp.where(b == z, 1.0, 0.0) * self.part[...]
                for d in range(1, N_BLK):
                    term += jnp.where(lax.rem(b + d, N_BLK) == z, 1.0, 0.0) * self.zbuf[d - 1]
                total += term
            self.mid[...] = total
            self.res[pl.ds(pl.multiple_of(g * self.rows, self.rows), self.rows)] = total
            self.each(lambda i: self.share(i).start())

        def finish(self):
            self.each(lambda i: self.share(i).wait())

    reduce1 = Reduce(x1, buf1, part1, zbuf1, mid1, grams1, red1_sem, zred1_sem)
    reduce2 = Reduce(x2, buf2, part2, zbuf2, mid2, grams2, red2_sem, zred2_sem)

    per = 8
    back = 12
    rows_at_once = 8

    def operate(stage, fv, out, x_h, x_y, x_at, trm, fet):
        if stage == 0:
            loads[0].wait()
        halo_copies = [
            remote(fv.at[pl.ds(0, HB)], halo.at[stage, pl.ds(HB, HB)],
                   halo_send.at[stage, 0], halo_recv.at[stage, 0], left),
            remote(fv.at[pl.ds(brows - HB, HB)], halo.at[stage, pl.ds(0, HB)],
                   halo_send.at[stage, 1], halo_recv.at[stage, 1], right),
        ]

        for d in range(N_BLK):
            for s in range(SHORT):
                if d == 0:
                    fet[s] = fv[wanted[s]]
                else:
                    fet_out[(d - 1) * SHORT + s] = fv[wanted[d * SHORT + s]]
        fet_copies = [
            remote(fet_out.at[pl.ds((d - 1) * SHORT, SHORT)], fet.at[pl.ds((4 - d) * SHORT, SHORT)],
                   fet_send.at[stage, d - 1], fet_recv.at[stage, 3 - d], peers[d])
            for d in (1, 3, 2)
        ]

        def split_own(i, c):
            for u in range(4):
                r = i * 4 + u
                hi, lo = split(fv[r])
                ext[HB + r, :128, :] = hi
                ext[HB + r, 128:, :] = lo
            return c

        lax.fori_loop(0, brows // 4, split_own, 0)

        if stage == 0:
            loads[1].wait()
        terms = []
        for d in range(N_BLK):
            c = lax.rem(b + d, N_BLK)
            for s in range(SHORT):
                terms.append(three(ws[c * SHORT + s].T, ext[HB + srows[c, s]]))
        for s in range(SHORT):
            trm[s] = terms[s]
        for i in range(SHORT, N_BLK * SHORT):
            trm_out[i - SHORT] = terms[i]
        trm_copies = [
            remote(trm_out.at[pl.ds((d - 1) * SHORT, SHORT)], trm.at[pl.ds((4 - d) * SHORT, SHORT)],
                   trm_send.at[stage, d - 1], trm_recv.at[stage, 3 - d], peers[d])
            for d in (1, 3, 2)
        ]

        if stage == 0:
            loads[2].wait()

        def backward(i, carry):
            terms = []
            for u in range(back):
                m = plan[PERM, i * back + u]
                terms.append(three(wn[m].T, ext[HB + lax.div(m, NEAR_PER)]))
            run = seg[i * back]
            for u in range(back):
                run = run * plan[KEEP, i * back + u].astype(F32) + terms[u]
                seg[i * back + u + 1] = run
            return carry

        lax.fori_loop(0, brows * NEAR_PER // back, backward, 0)
        for q in range(HB):
            rim_out[q] = seg[plan[LAST, q]]
            rim_out[HB + q] = seg[plan[LAST, HB + brows + q]]
        rim_copies = [
            remote(rim_out.at[pl.ds(0, HB)], rim_in.at[stage, pl.ds(HB, HB)],
                   rim_send.at[stage, 0], rim_recv.at[stage, 0], left),
            remote(rim_out.at[pl.ds(HB, HB)], rim_in.at[stage, pl.ds(0, HB)],
                   rim_send.at[stage, 1], rim_recv.at[stage, 1], right),
        ]

        acc_h[...] = jnp.zeros(acc_h.shape, F32)
        acc_l[...] = jnp.zeros(acc_l.shape, F32)
        acc_y[...] = jnp.zeros(acc_y.shape, F32)

        def halves(i):
            hi = ext[pl.ds(HB + i * per, per), :128, :].reshape(per * 128, 256)
            lo = ext[pl.ds(HB + i * per, per), 128:, :].reshape(per * 128, 256)
            return hi, lo

        def gram(i, c):
            hi, lo = halves(i)
            both = dot_t(hi, jnp.concatenate([hi, lo], axis=1))
            acc_h[...] += both[:, :256] + dot_t(lo, lo)
            acc_l[...] += both[:, 256:]
            return c

        lax.fori_loop(0, brows // per, gram, 0)
        low = acc_l[...]
        x_h[pl.ds(x_at, 256)] = acc_h[...] + (low + low.T)
        if stage == 1:
            reduce1.scatter()

        for copy in halo_copies:
            copy.wait()
        for q in range(2 * HB):
            hi, lo = split(halo[stage, q])
            at = q if q < HB else q + brows
            ext[at, :128, :] = hi
            ext[at, 128:, :] = lo

        def half_diag(r):
            d = dsp[r]
            return jnp.concatenate([d, d], axis=1) * fv[r]

        def forward(i, c):
            sums = []
            for u in range(rows_at_once):
                lhs, rhs = [], []
                for j in range(NEAR_PER):
                    m = (i * rows_at_once + u) * NEAR_PER + j
                    hi, lo = split(wn[m])
                    e = ext[cols[m]]
                    lhs += [hi, hi, lo]
                    rhs += [e, e[:128]]
                sums.append(dot(jnp.concatenate(lhs, axis=1), jnp.concatenate(rhs, axis=0)))
            for u in range(rows_at_once):
                r = i * rows_at_once + u
                out[r] = half_diag(r) + sums[u]
            return c

        lax.fori_loop(0, brows // rows_at_once, forward, 0)
        if stage == 1:
            reduce1.across()

        for copy in fet_copies:
            copy.wait()
        terms = []
        for i in range(N_BLK * SHORT):
            n = plan[SPERM, i]
            slot = lax.rem(lax.div(n, SHORT) + N_BLK - b, N_BLK) * SHORT + lax.rem(n, SHORT)
            hi, lo = split(fet[slot])
            terms.append(three(ws[n], jnp.concatenate([hi, lo], axis=0)))
        run = rseg[0]
        for i in range(N_BLK * SHORT):
            run = run * plan[SKEEP, i].astype(F32) + terms[i]
            rseg[i + 1] = run

        def gram_y(i, c):
            parts = []
            for u in range(per):
                r = i * per + u
                f = out[r] + rseg[plan[SLAST, r]]
                out[r] = f
                parts.append(f)
            fh, fl = split(jnp.concatenate(parts, axis=0))
            hi, lo = halves(i)
            both = dot_t(hi, jnp.concatenate([fh, fl], axis=1))
            acc_y[...] += (both[:, :256] + both[:, 256:]) + dot_t(lo, fh)
            return c

        lax.fori_loop(0, brows // per, gram_y, 0)
        y = acc_y[...]
        x_y[pl.ds(256 if stage == 0 else 0, 256)] = y + y.T
        if stage == 1:
            reduce2.scatter()
            reduce1.gather()

        for copy in trm_copies:
            copy.wait()
        run = tseg[0]
        for i in range(N_BLK * SHORT):
            run = run * tplan[KEEP, i].astype(F32) + trm[tplan[PERM, i]]
            tseg[i + 1] = run

        def finish(i, c):
            for u in range(4):
                r = i * 4 + u
                out[r] = (out[r] + half_diag(r)) + (seg[plan[LAST, HB + r]] + tseg[tplan[LAST, r]])
            return c

        if stage == 1:
            reduce2.across()
        lax.fori_loop(0, brows // 4, finish, 0)
        if stage == 1:
            reduce2.gather()
        for copy in rim_copies:
            copy.wait()
        for q in range(HB):
            out[q] = out[q] + rim_in[stage, q]
            out[brows - HB + q] = out[brows - HB + q] + rim_in[stage, HB + q]

    operate(0, f0, f1, x1, x1, 0, trm_0, fet_0)
    copy1 = pltpu.make_async_copy(f1, image, out_sem.at[0])
    copy1.start()
    operate(1, f1, f0, x1, x2, 512, trm_1, fet_1)
    copy2 = pltpu.make_async_copy(f0, image2, out_sem.at[1])
    copy2.start()
    reduce1.finish()
    reduce2.finish()
    copy1.wait()
    copy2.wait()


def krylov(near_cols, short_rows, short_cols, field, diag, near, short):
    brows = field.shape[0]
    smem = pl.BlockSpec(memory_space=pltpu.SMEM)
    vmem = pl.BlockSpec(memory_space=pltpu.VMEM)
    hbm = pl.BlockSpec(memory_space=pl.ANY)
    n_grp = 32
    dma = pltpu.SemaphoreType.DMA

    def block(*n):
        return pltpu.VMEM(n + (128, 256), F32)

    def words(*n):
        return pltpu.VMEM(n + (8, 128), jnp.int32)

    def reduce_scratch(rows):
        piece = rows // n_grp
        return [
            pltpu.VMEM((rows, 256), F32), pltpu.VMEM((n_grp - 1, piece, 256), F32), pltpu.VMEM((piece, 256), F32),
            pltpu.VMEM((N_BLK - 1, piece, 256), F32), pltpu.VMEM((piece, 256), F32),
        ]

    return pl.pallas_call(
        krylov_kernel,
        out_shape=(
            jax.ShapeDtypeStruct(field.shape, F32),
            jax.ShapeDtypeStruct(field.shape, F32),
            jax.ShapeDtypeStruct((768, 256), F32),
            jax.ShapeDtypeStruct((256, 256), F32),
        ),
        in_specs=[smem, smem, smem, vmem, hbm, vmem, hbm, hbm],
        out_specs=(hbm, hbm, vmem, vmem),
        scratch_shapes=[
            block(brows), block(brows),
            pltpu.VMEM((brows + 2 * HB, 256, 256), BF16),
            pltpu.VMEM(near.shape, F32),
            pltpu.VMEM(short.shape, F32),
            pltpu.VMEM((brows, 128, 128), F32),
            block(brows * NEAR_PER + 1), block(9), block(9),
            block(2, 2 * HB), block(2 * HB), block(2, 2 * HB),
            block(6), block(8), block(8), block(6), block(8), block(8),
            words(), words(3), pltpu.SMEM((3, 8, 128), jnp.int32), words(),
            words(), pltpu.SMEM((8, 128), jnp.int32), words(), pltpu.SMEM((8, 128), jnp.int32),
            pltpu.VMEM((256, 256), F32), pltpu.VMEM((256, 256), F32), pltpu.VMEM((256, 256), F32),
            *reduce_scratch(768), *reduce_scratch(256),
            dma((3,)), dma((2,)), dma((3,)), dma((3,)), dma((3,)),
            dma((2, 2)), dma((2, 2)), dma((2, 3)), dma((2, 3)), dma((2, 3)), dma((2, 3)),
            dma((2, 2)), dma((2, 2)),
            dma((4, n_grp - 1)), dma((2, 3)), dma((4, n_grp - 1)), dma((2, 3)),
        ],
        compiler_params=pltpu.CompilerParams(
            collective_id=0, has_side_effects=True, vmem_limit_bytes=VMEM_LIMIT
        ),
        name="krylov",
    )(near_cols, short_rows, short_cols, near_cols.reshape(1, -1), field, diag, near, short)


def mm(a, b):
    return jnp.dot(a, b, precision=HIGHEST, preferred_element_type=F32)


def tail_kernel(
    grams1, grams2, r0, q1, s2, sol, res,
    rv, qv, sv, sol_v, res_v, w_sol, w_res, inv, err, load_sem, sol_sem, res_sem,
):
    loads = [
        pltpu.make_async_copy(src, dst, load_sem.at[i])
        for i, (src, dst) in enumerate(((r0, rv), (q1, qv), (s2, sv)))
    ]
    for copy in loads:
        copy.start()
    n = 256
    diagonal = lax.broadcasted_iota(jnp.int32, (n, n), 0) == lax.broadcasted_iota(jnp.int32, (n, n), 1)
    eye = jnp.where(diagonal, 1.0, 0.0)

    def scales(m):
        kept = jnp.where(diagonal, m, 0.0)
        return lax.rsqrt(jnp.sum(kept, axis=0, keepdims=True)), lax.rsqrt(jnp.sum(kept, axis=1, keepdims=True))

    def size(m):
        return jnp.max(jnp.abs(m))

    def square(limit):
        def step(state):
            e, x = err[...], inv[...]
            inv[...] = x + mm(x, e)
            e = mm(e, e)
            err[...] = e
            return state[0] + 1, size(e)

        return lax.while_loop(
            lambda state: (state[0] < limit) & (state[1] > 1e-5), step, (jnp.int32(0), size(err[...]))
        )[1]

    def polish(m):
        def step(state):
            x = inv[...]
            e = eye - mm(m, x)
            inv[...] = x + mm(x, e)
            return state[0] + 1, size(e)

        lax.while_loop(lambda state: (state[0] < 6) & (state[1] > 1e-5), step, (jnp.int32(0), F32(1.0)))

    def spd_inverse(m, guess):
        along, down = scales(m)
        scaled = m * along * down

        def from_norm():
            bound = jnp.max(jnp.sum(jnp.abs(scaled), axis=1, keepdims=True))
            start = eye / bound
            inv[...] = start
            err[...] = eye - scaled / bound
            square(48)

        if guess is None:
            from_norm()
        else:
            near = guess / along / down
            z = mm(scaled, near)
            tau = n / jnp.sum(jnp.where(diagonal, z, 0.0))
            inv[...] = near * tau
            err[...] = eye - z * tau
            left = square(6)

            @pl.when(jnp.logical_not(left <= 1e-5))
            def _():
                from_norm()

        polish(scaled)
        return inv[...] * along * down

    def solve(matrix, inverse, rhs):
        x = mm(inverse, rhs)
        return x + mm(inverse, rhs - mm(matrix, x))

    rr0, g01, g11 = (grams1[i * n : (i + 1) * n, :] for i in range(3))
    g12 = grams2[...]
    inv0 = spd_inverse(rr0, None)
    a1 = solve(g01, spd_inverse(g01, inv0), rr0)
    ga = mm(g01, a1)
    g11a = mm(g11, a1)
    rr1 = (rr0 - ga) + (mm(a1.T, g11a) - ga.T)
    rr1 = 0.5 * (rr1 + rr1.T)
    t = eye + solve(rr0, inv0, rr1)
    cross = mm(t.T, g11a)
    pq2 = (mm(t.T, mm(g01, t)) - cross) + (mm(a1.T, mm(g12, a1)) - cross.T)
    pq2 = 0.5 * (pq2 + pq2.T)
    a2 = solve(pq2, spd_inverse(pq2, inv0), rr1)
    c_hi, c_lo = split(a1 + mm(t, a2))
    d_hi, d_lo = split(mm(a1, a2))
    for i, part in enumerate((c_hi, c_lo, c_hi, -d_hi, -d_lo, -d_hi)):
        w_sol[i * n : (i + 1) * n, :] = part
        w_res[i * n : (i + 1) * n, :] = -part

    for copy in loads:
        copy.wait()
    tile = 512
    tiles = rv.shape[0] // tile

    def three(x, y):
        x_hi, x_lo = split(x)
        y_hi, y_lo = split(y)
        return jnp.concatenate([x_hi, x_hi, x_lo, y_hi, y_hi, y_lo], axis=1)

    for i in range(tiles):
        at = pl.ds(i * tile, tile)
        sol_v[at] = dot(three(rv[at], qv[at]), w_sol[...])
        pltpu.make_async_copy(sol_v.at[at], sol.at[at], sol_sem.at[i]).start()
        res_v[at] = rv[at] + dot(three(qv[at], sv[at]), w_res[...])
        pltpu.make_async_copy(res_v.at[at], res.at[at], res_sem.at[i]).start()
    for i in range(tiles):
        at = pl.ds(i * tile, tile)
        pltpu.make_async_copy(sol_v.at[at], sol.at[at], sol_sem.at[i]).wait()
        pltpu.make_async_copy(res_v.at[at], res.at[at], res_sem.at[i]).wait()


def tail(grams1, grams2, r0, q1, s2):
    vmem = pl.BlockSpec(memory_space=pltpu.VMEM)
    hbm = pl.BlockSpec(memory_space=pl.ANY)
    dma = pltpu.SemaphoreType.DMA
    field = pltpu.VMEM(r0.shape, F32)
    return pl.pallas_call(
        tail_kernel,
        out_shape=(jax.ShapeDtypeStruct(r0.shape, F32),) * 2,
        in_specs=[vmem, vmem, hbm, hbm, hbm],
        out_specs=(hbm, hbm),
        scratch_shapes=[
            field, field, field, field, field,
            pltpu.VMEM((1536, 256), BF16), pltpu.VMEM((1536, 256), BF16),
            pltpu.VMEM((256, 256), F32), pltpu.VMEM((256, 256), F32),
            dma((3,)), dma((8,)), dma((8,)),
        ],
        compiler_params=pltpu.CompilerParams(vmem_limit_bytes=VMEM_LIMIT),
        name="tail",
    )(grams1, grams2, r0, q1, s2)


def body(loads, pore_diag, near_blocks, near_cols, short_blocks, short_rows, short_cols):
    rows, cases = loads.shape
    brows = rows // 128
    q1, s2, grams1, grams2 = krylov(
        near_cols, short_rows, short_cols, loads.reshape(brows, 128, cases), pore_diag.reshape(brows, 128),
        near_blocks, short_blocks.reshape(-1, 128, 128),
    )
    return tail(grams1, grams2, loads, q1.reshape(rows, cases), s2.reshape(rows, cases))


def solution(mesh):
    in_specs = (
        P(("blk", "grp"), None),
        P(("blk", "grp")),
        P(("blk", "grp"), None, None),
        P(("blk", "grp")),
        P(("blk", "grp"), None, None, None),
        P(("blk", "grp"), None),
        P(("blk", "grp"), None),
    )
    out_specs = (P(("blk", "grp"), None), P(("blk", "grp"), None))
    return jax.shard_map(body, mesh=mesh, in_specs=in_specs, out_specs=out_specs, check_vma=False)
```

time: 912 us -> 133 us (0.15)
  waiting for transfers between devices: 363 us -> 0 us
  other arithmetic: 201 us -> 0 us
  matrix products: 190 us -> 0 us
  Pallas kernels: 0 us -> 129 us
  local copies, waits for them, and re-layouts: 101 us -> 2.67 us
  starting transfers between devices: 32 us -> 0 us
  between operations: 18.7 us -> 0.82 us
    psum x3 -> x0, waiting for transfers between devices: 363 us -> none  [summed(): return lax.psum(local, ('blk', 'grp'))]
    dot_general x23 -> x0, matrix products: 182 us -> none  [the longest x6 34.9 us: spread_rows(): return jnp.einsum('kq,kan->qan', selector, terms, precision=HIGH)]
    another operation x26 -> x0, other arithmetic: 163 us -> none  [the longest x19 103 us: chol_solve(): factor = jnp.linalg.cholesky(matrix)]
    pallas_call x0 -> x2, Pallas kernels: none -> 129 us  [the longest x1 93 us: krylov(): pl.pallas_call(krylov_kernel, out_shape=(jax.ShapeDtypeStruct(field.shape...]
    gather x8 -> x0, local copies, waits for them, and re-layouts: 36.2 us -> none  [the longest x2 22.3 us: operate(): partner = extended[near_cols].reshape(brows, NEAR_PER, block, cases)]
    all_to_all x5 -> x0, starting transfers between devices: 21.6 us -> none  [the longest x2 8.44 us: shortcut(): lax.all_to_all(fetch, 'blk', split_axis=0, concat_axis=0, tiled=True)]
    unnamed x42 -> x2, local copies, waits for them, and re-layouts: 19.9 us -> 2.67 us
    add x4 -> x0, other arithmetic: 16.7 us -> none  [the longest x2 14.3 us: operate(): own = own + shortcut(slab_blocks)]
  transfers between devices with their start and end apart: 16 -> 0, of which waited for: 3 -> 0; matrix products, arithmetic and copies ran while one was open for 25% -> 0% of each run, Pallas kernels for 0% -> 0%
where the time goes in v2:
time: 133 us; the launch traced here: 132 us
  Pallas kernels  129 us (97%)
  local copies, waits for them, and re-layouts  2.67 us (2%)
    pallas_call x1, Pallas kernels, krylov(): pl.pallas_call(krylov_kernel, out_shape=(jax.ShapeDtypeStruct(field.shape...  93 us
    pallas_call x1, Pallas kernels, tail(): pl.pallas_call(tail_kernel, out_shape=(jax.ShapeDtypeStruct(r0.shape, F32...  35.8 us
    unnamed x2, local copies, waits for them, and re-layouts  2.67 us

profile of v2, /device:TPU:1, one launch (start us, length us, event | category | flops | bytes accessed | tf_op | source)
XLA Modules:
  0.0 132.3 jit_solution(10968559247646933883)
XLA Ops:
  0.6 1.3 %copy.9.srows = s32[4,2]{1,0:T(4,128)} copy(s32[4,2]{0,1:T(2,128)} %param.12) | data formatting | bytes 64 | tf_op args[5]
  2.0 1.3 %copy.10.scols = s32[4,2]{1,0:T(4,128)} copy(s32[4,2]{0,1:T(2,128)} %param.13) | data formatting | bytes 64 | tf_op args[6]
  3.3 93.0 %krylov.1 = (f32[32,128,256]{2,1,0:T(8,128)}, f32[32,128,256]{2,1,0:T(8,128)}, f32[768,256]{1,0:T(8,128)}, f32[256,256]{1,0:T(8,128)}) custom-call(s32[96]{0:T(128)} %cols.1, s32[4,2]{1,0:T(4,128)} %copy.9.srows, s32[4,2]{1,0:T(4,128)} %copy.10.scols, s32[1,96]{1,0:T(1,128)} %bitcast.11, f32[32,128,256]{2,1,0:T(8,128)} %bitcast.6, f32[32,128]{1,0:T(8,128)} %bitcast.10, ...), custom_call_target="tpu_custom_call" | custom-call | tf_op jit(solution)/shard_map/krylov/pallas_call | solution.py:446
  96.3 35.8 %tail.1 = (f32[4096,256]{1,0:T(8,128)}, f32[4096,256]{1,0:T(8,128)}) custom-call(f32[768,256]{1,0:T(8,128)} %get-tuple-element.6.grams1, f32[256,256]{1,0:T(8,128)} %get-tuple-element.7.grams2, f32[4096,256]{1,0:T(8,128)} %r0.1, f32[4096,256]{1,0:T(8,128)} %bitcast.7, f32[4096,256]{1,0:T(8,128)} %bitcast.8), custom_call_target="tpu_custom_call" | custom-call | tf_op jit(solution)/shard_map/tail/pallas_call | solution.py:605

commit v3 on v2

--- a/solution.py
+++ b/solution.py
@@ -72,9 +72,9 @@
     image, image2, grams1, grams2,
     f0, f1, ext, wn, ws, dsp, seg, rseg, tseg, halo, rim_out, rim_in, trm_out, trm_0, trm_1, fet_out, fet_0, fet_1,
     tile, idx_in, idx_sm, keyrow, plan_v, plan, tplan_v, tplan, acc_h, acc_l, acc_y,
-    x1, buf1, part1, zbuf1, mid1, x2, buf2, part2, zbuf2, mid2,
+    x1, pair1, half1, buf1, part1, zbuf1, mid1, x2, buf2, part2, zbuf2, mid2,
     load_sem, out_sem, idx_sem, idx_send, idx_recv, halo_send, halo_recv, trm_send, trm_recv,
-    fet_send, fet_recv, rim_send, rim_recv, red1_sem, zred1_sem, red2_sem, zred2_sem,
+    fet_send, fet_recv, rim_send, rim_recv, pair_sem, red1_sem, zred1_sem, red2_sem, zred2_sem,
 ):
     brows = f0.shape[0]
     b = lax.axis_index("blk")
@@ -123,38 +123,22 @@
         remote(tile, idx_in.at[3 - d], idx_send.at[d - 1], idx_recv.at[3 - d], peers[d])
         for d in range(1, N_BLK)
     ]
-    keyrow[...] = jnp.zeros(keyrow.shape, jnp.int32)
-    keyrow[0:1, :96] = cols_row[...]
-    plan_v[...] = jnp.zeros(plan_v.shape, jnp.int32)
-    plan_v[0:1, :], plan_v[1:2, :], plan_v[2:3, :] = order(keyrow[0:1, :], 96)
-    plan_v[3:4, :], plan_v[4:5, :], plan_v[5:6, :] = order(
-        lanes([srows[c, s] for c in range(N_BLK) for s in range(SHORT)]), 8
-    )
-    plan_copy = pltpu.make_async_copy(plan_v, plan, idx_sem.at[0])
-    plan_copy.start()
-
-    def spread_diag(r, c):
-        dsp[r] = jnp.broadcast_to(diag[pl.ds(r, 1), :], (128, 128)).T * 0.5
-        return c
-
-    lax.fori_loop(0, brows, spread_diag, 0)
-    seg[0] = jnp.zeros(seg.shape[1:], F32)
-    rseg[0] = jnp.zeros(rseg.shape[1:], F32)
-    tseg[0] = jnp.zeros(tseg.shape[1:], F32)
     for copy in idx_copies:
         copy.wait()
     idx_copy = pltpu.make_async_copy(idx_in, idx_sm, idx_sem.at[1])
     idx_copy.start()
     idx_copy.wait()
-    tplan_v[...] = jnp.zeros(tplan_v.shape, jnp.int32)
     wanted = [scols[b, s] for s in range(SHORT)]
     for d in range(1, N_BLK):
         wanted += [idx_sm[d - 1, b, s] for s in range(SHORT)]
-    tplan_v[0:1, :], tplan_v[1:2, :], tplan_v[2:3, :] = order(lanes(wanted), 8)
-    tplan_copy = pltpu.make_async_copy(tplan_v, tplan, idx_sem.at[2])
-    tplan_copy.start()
-    plan_copy.wait()
-    tplan_copy.wait()
+    def sector_sum(part, zbuf):
+        total = jnp.zeros(part.shape, F32)
+        for z in range(N_BLK):
+            term = jnp.where(b == z, 1.0, 0.0) * part[...]
+            for d in range(1, N_BLK):
+                term += jnp.where(lax.rem(b + d, N_BLK) == z, 1.0, 0.0) * zbuf[d - 1]
+            total += term
+        return total
 
     class Reduce:
         def __init__(self, x, buf, part, zbuf, mid, res, sems, zsems):
@@ -205,12 +189,7 @@
         def gather(self):
             for copy in self.copies:
                 copy.wait()
-            total = jnp.zeros(self.part.shape, F32)
-            for z in range(N_BLK):
-                term = jnp.where(b == z, 1.0, 0.0) * self.part[...]
-                for d in range(1, N_BLK):
-                    term += jnp.where(lax.rem(b + d, N_BLK) == z, 1.0, 0.0) * self.zbuf[d - 1]
-                total += term
+            total = sector_sum(self.part, self.zbuf)
             self.mid[...] = total
             self.res[pl.ds(pl.multiple_of(g * self.rows, self.rows), self.rows)] = total
             self.each(lambda i: self.share(i).start())
@@ -218,12 +197,117 @@
         def finish(self):
             self.each(lambda i: self.share(i).wait())
 
-    reduce1 = Reduce(x1, buf1, part1, zbuf1, mid1, grams1, red1_sem, zred1_sem)
+    class PairReduce:
+        def __init__(self, x, pair, half, buf, part, zbuf, mid, res, psems, sems, zsems):
+            self.x, self.pair_in, self.half, self.buf = x, pair, half, buf
+            self.part, self.zbuf, self.mid, self.res = part, zbuf, mid, res
+            self.psems, self.sems, self.zsems = psems, sems, zsems
+            self.core, self.plane, self.planes = lax.rem(g, 2), lax.div(g, 2), n_grp // 2
+            self.other = (b, self.plane * 2 + 1 - self.core)
+            self.half_rows = x.shape[0] // 2
+            self.rows = self.half_rows // self.planes
+
+        def halved(self, ref, core):
+            return ref.at[pl.ds(pl.multiple_of(core * self.half_rows, self.half_rows), self.half_rows)]
+
+        def each(self, act):
+            def step(i, c):
+                act(i)
+                return c
+
+            lax.fori_loop(1, self.planes, step, 0)
+
+        def spread(self, i):
+            t = lax.rem(self.plane + i, self.planes)
+            return pltpu.make_async_remote_copy(
+                src_ref=self.half.at[pl.ds(pl.multiple_of(t * self.rows, self.rows), self.rows)],
+                dst_ref=self.buf.at[self.planes - 1 - i],
+                send_sem=self.sems.at[0, i - 1], recv_sem=self.sems.at[1, self.planes - 1 - i],
+                device_id=(b, t * 2 + self.core), device_id_type=MESH,
+            )
+
+        def own_piece(self):
+            at = self.core * self.half_rows + self.plane * self.rows
+            return pl.ds(pl.multiple_of(at, self.rows), self.rows)
+
+        def share(self, i):
+            t = lax.rem(self.plane + i, self.planes)
+            return pltpu.make_async_remote_copy(
+                src_ref=self.mid, dst_ref=self.res.at[self.own_piece()],
+                send_sem=self.sems.at[2, i - 1], recv_sem=self.sems.at[3, self.planes - 1 - i],
+                device_id=(b, t * 2 + self.core), device_id_type=MESH,
+            )
+
+        def pair(self):
+            self.paired = remote(
+                self.halved(self.x, 1 - self.core), self.pair_in, self.psems.at[0], self.psems.at[1], self.other
+            )
+
+        def scatter(self):
+            self.paired.wait()
+            at = pl.multiple_of(self.core * self.half_rows, self.half_rows)
+            self.half[...] = self.x[pl.ds(at, self.half_rows)] + self.pair_in[...]
+            self.each(lambda i: self.spread(i).start())
+
+        def across(self):
+            self.each(lambda i: self.spread(i).wait())
+            total = self.half[pl.ds(pl.multiple_of(self.plane * self.rows, self.rows), self.rows)]
+            for i in range(self.planes - 1):
+                total += self.buf[i]
+            self.part[...] = total
+            self.copies = [
+                remote(self.part, self.zbuf.at[3 - d], self.zsems.at[0, d - 1], self.zsems.at[1, 3 - d], peers[d])
+                for d in range(1, N_BLK)
+            ]
+
+        def gather(self):
+            for copy in self.copies:
+                copy.wait()
+            total = sector_sum(self.part, self.zbuf)
+            self.mid[...] = total
+            self.res[self.own_piece()] = total
+            self.each(lambda i: self.share(i).start())
+
+        def regroup(self):
+            self.each(lambda i: self.share(i).wait())
+            mine = self.halved(self.res, self.core)
+            self.paired = remote(mine, mine, self.psems.at[2], self.psems.at[3], self.other)
+
+        def finish(self):
+            self.paired.wait()
+
+    reduce1 = PairReduce(x1, pair1, half1, buf1, part1, zbuf1, mid1, grams1, pair_sem, red1_sem, zred1_sem)
     reduce2 = Reduce(x2, buf2, part2, zbuf2, mid2, grams2, red2_sem, zred2_sem)
 
     per = 8
     back = 12
     rows_at_once = 8
+
+    def make_plan():
+        keyrow[...] = jnp.zeros(keyrow.shape, jnp.int32)
+        keyrow[0:1, :96] = cols_row[...]
+        plan_v[...] = jnp.zeros(plan_v.shape, jnp.int32)
+        plan_v[0:1, :], plan_v[1:2, :], plan_v[2:3, :] = order(keyrow[0:1, :], 96)
+        plan_v[3:4, :], plan_v[4:5, :], plan_v[5:6, :] = order(
+            lanes([srows[c, s] for c in range(N_BLK) for s in range(SHORT)]), 8
+        )
+        plan_copy = pltpu.make_async_copy(plan_v, plan, idx_sem.at[0])
+        plan_copy.start()
+
+        def spread_diag(r, c):
+            dsp[r] = jnp.broadcast_to(diag[pl.ds(r, 1), :], (128, 128)).T * 0.5
+            return c
+
+        lax.fori_loop(0, brows, spread_diag, 0)
+        seg[0] = jnp.zeros(seg.shape[1:], F32)
+        rseg[0] = jnp.zeros(rseg.shape[1:], F32)
+        tseg[0] = jnp.zeros(tseg.shape[1:], F32)
+        tplan_v[...] = jnp.zeros(tplan_v.shape, jnp.int32)
+        tplan_v[0:1, :], tplan_v[1:2, :], tplan_v[2:3, :] = order(lanes(wanted), 8)
+        tplan_copy = pltpu.make_async_copy(tplan_v, tplan, idx_sem.at[2])
+        tplan_copy.start()
+        plan_copy.wait()
+        tplan_copy.wait()
 
     def operate(stage, fv, out, x_h, x_y, x_at, trm, fet):
         if stage == 0:
@@ -268,13 +352,42 @@
             trm[s] = terms[s]
         for i in range(SHORT, N_BLK * SHORT):
             trm_out[i - SHORT] = terms[i]
-        trm_copies = [
-            remote(trm_out.at[pl.ds((d - 1) * SHORT, SHORT)], trm.at[pl.ds((4 - d) * SHORT, SHORT)],
-                   trm_send.at[stage, d - 1], trm_recv.at[stage, 3 - d], peers[d])
-            for d in (1, 3, 2)
-        ]
-
+
+        def send_terms(s):
+            return [
+                remote(trm_out.at[(d - 1) * SHORT + s], trm.at[(4 - d) * SHORT + s],
+                       trm_send.at[stage, s, d - 1], trm_recv.at[stage, s, 3 - d], peers[d])
+                for d in (1, 3, 2)
+            ]
+
+        trm_copies = send_terms(0)
         if stage == 0:
+            trm_copies += send_terms(1)
+
+        acc_h[...] = jnp.zeros(acc_h.shape, F32)
+        acc_l[...] = jnp.zeros(acc_l.shape, F32)
+        acc_y[...] = jnp.zeros(acc_y.shape, F32)
+
+        def halves(i):
+            hi = ext[pl.ds(HB + i * per, per), :128, :].reshape(per * 128, 256)
+            lo = ext[pl.ds(HB + i * per, per), 128:, :].reshape(per * 128, 256)
+            return hi, lo
+
+        def gram(i, c):
+            hi, lo = halves(i)
+            both = dot_t(hi, jnp.concatenate([hi, lo], axis=1))
+            acc_h[...] += both[:, :256] + dot_t(lo, lo)
+            acc_l[...] += both[:, 256:]
+            return c
+
+        lax.fori_loop(0, brows // per, gram, 0)
+        low = acc_l[...]
+        x_h[pl.ds(x_at, 256)] = acc_h[...] + (low + low.T)
+        if stage == 1:
+            reduce1.pair()
+
+        if stage == 0:
+            make_plan()
             loads[2].wait()
 
         def backward(i, carry):
@@ -298,26 +411,6 @@
             remote(rim_out.at[pl.ds(HB, HB)], rim_in.at[stage, pl.ds(0, HB)],
                    rim_send.at[stage, 1], rim_recv.at[stage, 1], right),
         ]
-
-        acc_h[...] = jnp.zeros(acc_h.shape, F32)
-        acc_l[...] = jnp.zeros(acc_l.shape, F32)
-        acc_y[...] = jnp.zeros(acc_y.shape, F32)
-
-        def halves(i):
-            hi = ext[pl.ds(HB + i * per, per), :128, :].reshape(per * 128, 256)
-            lo = ext[pl.ds(HB + i * per, per), 128:, :].reshape(per * 128, 256)
-            return hi, lo
-
-        def gram(i, c):
-            hi, lo = halves(i)
-            both = dot_t(hi, jnp.concatenate([hi, lo], axis=1))
-            acc_h[...] += both[:, :256] + dot_t(lo, lo)
-            acc_l[...] += both[:, 256:]
-            return c
-
-        lax.fori_loop(0, brows // per, gram, 0)
-        low = acc_l[...]
-        x_h[pl.ds(x_at, 256)] = acc_h[...] + (low + low.T)
         if stage == 1:
             reduce1.scatter()
 
@@ -352,6 +445,7 @@
         lax.fori_loop(0, brows // rows_at_once, forward, 0)
         if stage == 1:
             reduce1.across()
+            trm_copies += send_terms(1)
 
         for copy in fet_copies:
             copy.wait()
@@ -403,7 +497,7 @@
             reduce2.across()
         lax.fori_loop(0, brows // 4, finish, 0)
         if stage == 1:
-            reduce2.gather()
+            reduce1.regroup()
         for copy in rim_copies:
             copy.wait()
         for q in range(HB):
@@ -416,6 +510,7 @@
     operate(1, f1, f0, x1, x2, 512, trm_1, fet_1)
     copy2 = pltpu.make_async_copy(f0, image2, out_sem.at[1])
     copy2.start()
+    reduce2.gather()
     reduce1.finish()
     reduce2.finish()
     copy1.wait()
@@ -436,10 +531,9 @@
     def words(*n):
         return pltpu.VMEM(n + (8, 128), jnp.int32)
 
-    def reduce_scratch(rows):
-        piece = rows // n_grp
+    def reduce_scratch(n, piece):
         return [
-            pltpu.VMEM((rows, 256), F32), pltpu.VMEM((n_grp - 1, piece, 256), F32), pltpu.VMEM((piece, 256), F32),
+            pltpu.VMEM((n - 1, piece, 256), F32), pltpu.VMEM((piece, 256), F32),
             pltpu.VMEM((N_BLK - 1, piece, 256), F32), pltpu.VMEM((piece, 256), F32),
         ]
 
@@ -465,11 +559,13 @@
             words(), words(3), pltpu.SMEM((3, 8, 128), jnp.int32), words(),
             words(), pltpu.SMEM((8, 128), jnp.int32), words(), pltpu.SMEM((8, 128), jnp.int32),
             pltpu.VMEM((256, 256), F32), pltpu.VMEM((256, 256), F32), pltpu.VMEM((256, 256), F32),
-            *reduce_scratch(768), *reduce_scratch(256),
+            pltpu.VMEM((768, 256), F32), pltpu.VMEM((384, 256), F32), pltpu.VMEM((384, 256), F32),
+            *reduce_scratch(16, 24),
+            pltpu.VMEM((256, 256), F32), *reduce_scratch(32, 8),
             dma((3,)), dma((2,)), dma((3,)), dma((3,)), dma((3,)),
-            dma((2, 2)), dma((2, 2)), dma((2, 3)), dma((2, 3)), dma((2, 3)), dma((2, 3)),
+            dma((2, 2)), dma((2, 2)), dma((2, 2, 3)), dma((2, 2, 3)), dma((2, 3)), dma((2, 3)),
             dma((2, 2)), dma((2, 2)),
-            dma((4, n_grp - 1)), dma((2, 3)), dma((4, n_grp - 1)), dma((2, 3)),
+            dma((4,)), dma((4, n_grp // 2 - 1)), dma((2, 3)), dma((4, n_grp - 1)), dma((2, 3)),
         ],
         compiler_params=pltpu.CompilerParams(
             collective_id=0, has_side_effects=True, vmem_limit_bytes=VMEM_LIMIT
@@ -482,9 +578,13 @@
     return jnp.dot(a, b, precision=HIGHEST, preferred_element_type=F32)
 
 
+def mm3(a, b):
+    return jnp.dot(a, b, precision=lax.Precision.HIGH, preferred_element_type=F32)
+
+
 def tail_kernel(
     grams1, grams2, r0, q1, s2, sol, res,
-    rv, qv, sv, sol_v, res_v, w_sol, w_res, inv, err, load_sem, sol_sem, res_sem,
+    rv, qv, sv, sol_v, res_v, w_sol, w_res, work, load_sem, sol_sem, res_sem,
 ):
     loads = [
         pltpu.make_async_copy(src, dst, load_sem.at[i])
@@ -505,24 +605,24 @@
 
     def square(limit):
         def step(state):
-            e, x = err[...], inv[...]
-            inv[...] = x + mm(x, e)
-            e = mm(e, e)
-            err[...] = e
-            return state[0] + 1, size(e)
+            e = work[n:, :]
+            both = mm3(work[...], e)
+            work[:n, :] = work[:n, :] + both[:n]
+            work[n:, :] = both[n:]
+            return state[0] + 1, size(both[n:])
 
         return lax.while_loop(
-            lambda state: (state[0] < limit) & (state[1] > 1e-5), step, (jnp.int32(0), size(err[...]))
+            lambda state: (state[0] < limit) & (state[1] > 1e-5), step, (jnp.int32(0), size(work[n:, :]))
         )[1]
 
     def polish(m):
         def step(state):
-            x = inv[...]
+            x = work[:n, :]
             e = eye - mm(m, x)
-            inv[...] = x + mm(x, e)
+            work[:n, :] = x + mm(x, e)
             return state[0] + 1, size(e)
 
-        lax.while_loop(lambda state: (state[0] < 6) & (state[1] > 1e-5), step, (jnp.int32(0), F32(1.0)))
+        lax.while_loop(lambda state: (state[0] < 6) & (state[1] > 1e-4), step, (jnp.int32(0), F32(1.0)))
 
     def spd_inverse(m, guess):
         along, down = scales(m)
@@ -530,10 +630,10 @@
 
         def from_norm():
             bound = jnp.max(jnp.sum(jnp.abs(scaled), axis=1, keepdims=True))
-            start = eye / bound
-            inv[...] = start
-            err[...] = eye - scaled / bound
+            work[:n, :] = eye / bound
+            work[n:, :] = eye - scaled / bound
             square(48)
+            polish(scaled)
 
         if guess is None:
             from_norm()
@@ -541,20 +641,19 @@
             near = guess / along / down
             z = mm(scaled, near)
             tau = n / jnp.sum(jnp.where(diagonal, z, 0.0))
-            inv[...] = near * tau
-            err[...] = eye - z * tau
+            work[:n, :] = near * tau
+            work[n:, :] = eye - z * tau
             left = square(6)
 
             @pl.when(jnp.logical_not(left <= 1e-5))
             def _():
                 from_norm()
 
-        polish(scaled)
-        return inv[...] * along * down
+        return work[:n, :] * along * down
 
     def solve(matrix, inverse, rhs):
-        x = mm(inverse, rhs)
-        return x + mm(inverse, rhs - mm(matrix, x))
+        x = mm3(inverse, rhs)
+        return x + mm3(inverse, rhs - mm(matrix, x))
 
     rr0, g01, g11 = (grams1[i * n : (i + 1) * n, :] for i in range(3))
     g12 = grams2[...]
@@ -569,8 +668,12 @@
     pq2 = (mm(t.T, mm(g01, t)) - cross) + (mm(a1.T, mm(g12, a1)) - cross.T)
     pq2 = 0.5 * (pq2 + pq2.T)
     a2 = solve(pq2, spd_inverse(pq2, inv0), rr1)
-    c_hi, c_lo = split(a1 + mm(t, a2))
-    d_hi, d_lo = split(mm(a1, a2))
+    c = a1 + mm(t, a2)
+    d = mm(a1, a2)
+    c_diag = jnp.sum(jnp.where(diagonal, c, 0.0), axis=0, keepdims=True)
+    d_diag = jnp.sum(jnp.where(diagonal, d, 0.0), axis=0, keepdims=True)
+    c_hi, c_lo = split(jnp.where(diagonal, 0.0, c))
+    d_hi, d_lo = split(jnp.where(diagonal, 0.0, d))
     for i, part in enumerate((c_hi, c_lo, c_hi, -d_hi, -d_lo, -d_hi)):
         w_sol[i * n : (i + 1) * n, :] = part
         w_res[i * n : (i + 1) * n, :] = -part
@@ -587,9 +690,9 @@
 
     for i in range(tiles):
         at = pl.ds(i * tile, tile)
-        sol_v[at] = dot(three(rv[at], qv[at]), w_sol[...])
+        sol_v[at] = (rv[at] * c_diag - qv[at] * d_diag) + dot(three(rv[at], qv[at]), w_sol[...])
         pltpu.make_async_copy(sol_v.at[at], sol.at[at], sol_sem.at[i]).start()
-        res_v[at] = rv[at] + dot(three(qv[at], sv[at]), w_res[...])
+        res_v[at] = (rv[at] - qv[at] * c_diag + sv[at] * d_diag) + dot(three(qv[at], sv[at]), w_res[...])
         pltpu.make_async_copy(res_v.at[at], res.at[at], res_sem.at[i]).start()
     for i in range(tiles):
         at = pl.ds(i * tile, tile)
@@ -610,7 +713,7 @@
         scratch_shapes=[
             field, field, field, field, field,
             pltpu.VMEM((1536, 256), BF16), pltpu.VMEM((1536, 256), BF16),
-            pltpu.VMEM((256, 256), F32), pltpu.VMEM((256, 256), F32),
+            pltpu.VMEM((512, 256), F32),
             dma((3,)), dma((8,)), dma((8,)),
         ],
         compiler_params=pltpu.CompilerParams(vmem_limit_bytes=VMEM_LIMIT),

time: 133 us -> 118 us (0.89)
  Pallas kernels: 129 us -> 114 us
    pallas_call x1, Pallas kernels: 93 us -> 84.5 us  [krylov(): pl.pallas_call(krylov_kernel, out_shape=(jax.ShapeDtypeStruct(field.shape...]
    pallas_call x1, Pallas kernels: 35.8 us -> 29.6 us  [tail(): pl.pallas_call(tail_kernel, out_shape=(jax.ShapeDtypeStruct(r0.shape, F32...]
where the time goes in v3:
time: 118 us
  Pallas kernels  114 us (97%)
  local copies, waits for them, and re-layouts  2.67 us (2%)
    pallas_call x1, Pallas kernels, krylov(): pl.pallas_call(krylov_kernel, out_shape=(jax.ShapeDtypeStruct(field.shape...  84.5 us
    pallas_call x1, Pallas kernels, tail(): pl.pallas_call(tail_kernel, out_shape=(jax.ShapeDtypeStruct(r0.shape, F32...  29.6 us
    unnamed x2, local copies, waits for them, and re-layouts  2.67 us

profile of v3, /device:TPU:1, one launch (start us, length us, event | category | flops | bytes accessed | tf_op | source)
XLA Modules:
  0.0 117.7 jit_solution(6330249240650974243)
XLA Ops:
  0.6 1.3 %copy.9.srows = s32[4,2]{1,0:T(4,128)} copy(s32[4,2]{0,1:T(2,128)} %param.12) | data formatting | bytes 64 | tf_op args[5]
  2.0 1.3 %copy.10.scols = s32[4,2]{1,0:T(4,128)} copy(s32[4,2]{0,1:T(2,128)} %param.13) | data formatting | bytes 64 | tf_op args[6]
  3.3 84.5 %krylov.1 = (f32[32,128,256]{2,1,0:T(8,128)}, f32[32,128,256]{2,1,0:T(8,128)}, f32[768,256]{1,0:T(8,128)}, f32[256,256]{1,0:T(8,128)}) custom-call(s32[96]{0:T(128)} %cols.1, s32[4,2]{1,0:T(4,128)} %copy.9.srows, s32[4,2]{1,0:T(4,128)} %copy.10.scols, s32[1,96]{1,0:T(1,128)} %bitcast.11, f32[32,128,256]{2,1,0:T(8,128)} %bitcast.6, f32[32,128]{1,0:T(8,128)} %bitcast.10, ...), custom_call_target="tpu_custom_call" | custom-call | tf_op jit(solution)/shard_map/krylov/pallas_call | solution.py:540
  87.9 29.6 %tail.1 = (f32[4096,256]{1,0:T(8,128)}, f32[4096,256]{1,0:T(8,128)}) custom-call(f32[768,256]{1,0:T(8,128)} %get-tuple-element.6.grams1, f32[256,256]{1,0:T(8,128)} %get-tuple-element.7.grams2, f32[4096,256]{1,0:T(8,128)} %r0.1, f32[4096,256]{1,0:T(8,128)} %bitcast.7, f32[4096,256]{1,0:T(8,128)} %bitcast.8), custom_call_target="tpu_custom_call" | custom-call | tf_op jit(solution)/shard_map/tail/pallas_call | solution.py:708

commit v4 on v3

--- a/solution.py
+++ b/solution.py
@@ -116,21 +116,32 @@
     own = jnp.zeros((8, 128), jnp.int32)
     for c in range(N_BLK):
         for s in range(SHORT):
-            own = jnp.where((sub == c) & (lane == s), scols[c, s], own)
+            own = jnp.where((sub == c) & (lane == s), scols[s, c], own)
     tile[...] = own
+    keyrow[...] = jnp.zeros(keyrow.shape, jnp.int32)
+    keyrow[0:1, :96] = cols_row[...]
+    plan_v[...] = jnp.zeros(plan_v.shape, jnp.int32)
+    plan_v[0:1, :], plan_v[1:2, :], plan_v[2:3, :] = order(keyrow[0:1, :], 96)
+    plan_v[3:4, :], plan_v[4:5, :], plan_v[5:6, :] = order(
+        lanes([srows[s, c] for c in range(N_BLK) for s in range(SHORT)]), 8
+    )
+    plan_copy = pltpu.make_async_copy(plan_v, plan, idx_sem.at[0])
+    plan_copy.start()
+
+    def spread_diag(r, c):
+        dsp[r] = jnp.broadcast_to(diag[pl.ds(r, 1), :], (128, 128)).T * 0.5
+        return c
+
+    lax.fori_loop(0, brows, spread_diag, 0)
+    seg[0] = jnp.zeros(seg.shape[1:], F32)
+    rseg[0] = jnp.zeros(rseg.shape[1:], F32)
+    tseg[0] = jnp.zeros(tseg.shape[1:], F32)
     pl.semaphore_wait(barrier, n_grp - 1 + N_BLK - 1)
     idx_copies = [
         remote(tile, idx_in.at[3 - d], idx_send.at[d - 1], idx_recv.at[3 - d], peers[d])
         for d in range(1, N_BLK)
     ]
-    for copy in idx_copies:
-        copy.wait()
-    idx_copy = pltpu.make_async_copy(idx_in, idx_sm, idx_sem.at[1])
-    idx_copy.start()
-    idx_copy.wait()
-    wanted = [scols[b, s] for s in range(SHORT)]
-    for d in range(1, N_BLK):
-        wanted += [idx_sm[d - 1, b, s] for s in range(SHORT)]
+
     def sector_sum(part, zbuf):
         total = jnp.zeros(part.shape, F32)
         for z in range(N_BLK):
@@ -283,31 +294,22 @@
     back = 12
     rows_at_once = 8
 
-    def make_plan():
-        keyrow[...] = jnp.zeros(keyrow.shape, jnp.int32)
-        keyrow[0:1, :96] = cols_row[...]
-        plan_v[...] = jnp.zeros(plan_v.shape, jnp.int32)
-        plan_v[0:1, :], plan_v[1:2, :], plan_v[2:3, :] = order(keyrow[0:1, :], 96)
-        plan_v[3:4, :], plan_v[4:5, :], plan_v[5:6, :] = order(
-            lanes([srows[c, s] for c in range(N_BLK) for s in range(SHORT)]), 8
-        )
-        plan_copy = pltpu.make_async_copy(plan_v, plan, idx_sem.at[0])
-        plan_copy.start()
-
-        def spread_diag(r, c):
-            dsp[r] = jnp.broadcast_to(diag[pl.ds(r, 1), :], (128, 128)).T * 0.5
-            return c
-
-        lax.fori_loop(0, brows, spread_diag, 0)
-        seg[0] = jnp.zeros(seg.shape[1:], F32)
-        rseg[0] = jnp.zeros(rseg.shape[1:], F32)
-        tseg[0] = jnp.zeros(tseg.shape[1:], F32)
+    def learn_wanted():
+        for copy in idx_copies:
+            copy.wait()
+        idx_copy = pltpu.make_async_copy(idx_in, idx_sm, idx_sem.at[1])
+        idx_copy.start()
+        idx_copy.wait()
+        wanted = [scols[s, b] for s in range(SHORT)]
+        for d in range(1, N_BLK):
+            wanted += [idx_sm[d - 1, b, s] for s in range(SHORT)]
         tplan_v[...] = jnp.zeros(tplan_v.shape, jnp.int32)
         tplan_v[0:1, :], tplan_v[1:2, :], tplan_v[2:3, :] = order(lanes(wanted), 8)
         tplan_copy = pltpu.make_async_copy(tplan_v, tplan, idx_sem.at[2])
         tplan_copy.start()
-        plan_copy.wait()
-        tplan_copy.wait()
+        return wanted, tplan_copy
+
+    known = []
 
     def operate(stage, fv, out, x_h, x_y, x_at, trm, fet):
         if stage == 0:
@@ -319,17 +321,46 @@
                    halo_send.at[stage, 1], halo_recv.at[stage, 1], right),
         ]
 
+        def send_fetch(wanted):
+            for d in range(N_BLK):
+                for s in range(SHORT):
+                    if d == 0:
+                        fet[s] = fv[wanted[s]]
+                    else:
+                        fet_out[(d - 1) * SHORT + s] = fv[wanted[d * SHORT + s]]
+            return [
+                remote(fet_out.at[pl.ds((d - 1) * SHORT, SHORT)], fet.at[pl.ds((4 - d) * SHORT, SHORT)],
+                       fet_send.at[stage, d - 1], fet_recv.at[stage, 3 - d], peers[d])
+                for d in (1, 3, 2)
+            ]
+
+        if stage == 1:
+            fet_copies = send_fetch(known[0])
+
+        if stage == 0:
+            loads[1].wait()
+        terms = []
         for d in range(N_BLK):
+            c = lax.rem(b + d, N_BLK)
             for s in range(SHORT):
-                if d == 0:
-                    fet[s] = fv[wanted[s]]
-                else:
-                    fet_out[(d - 1) * SHORT + s] = fv[wanted[d * SHORT + s]]
-        fet_copies = [
-            remote(fet_out.at[pl.ds((d - 1) * SHORT, SHORT)], fet.at[pl.ds((4 - d) * SHORT, SHORT)],
-                   fet_send.at[stage, d - 1], fet_recv.at[stage, 3 - d], peers[d])
-            for d in (1, 3, 2)
-        ]
+                terms.append(three(ws[c * SHORT + s].T, jnp.concatenate(split(fv[srows[s, c]]), axis=0)))
+        for s in range(SHORT):
+            trm[s] = terms[s]
+        for i in range(SHORT, N_BLK * SHORT):
+            trm_out[i - SHORT] = terms[i]
+
+        def send_terms(s):
+            return [
+                remote(trm_out.at[(d - 1) * SHORT + s], trm.at[(4 - d) * SHORT + s],
+                       trm_send.at[stage, s, d - 1], trm_recv.at[stage, s, 3 - d], peers[d])
+                for d in (1, 3, 2)
+            ]
+
+        trm_copies = send_terms(0)
+        trm_copies += send_terms(1)
+        if stage == 0:
+            known.extend(learn_wanted())
+            fet_copies = send_fetch(known[0])
 
         def split_own(i, c):
             for u in range(4):
@@ -341,29 +372,6 @@
 
         lax.fori_loop(0, brows // 4, split_own, 0)
 
-        if stage == 0:
-            loads[1].wait()
-        terms = []
-        for d in range(N_BLK):
-            c = lax.rem(b + d, N_BLK)
-            for s in range(SHORT):
-                terms.append(three(ws[c * SHORT + s].T, ext[HB + srows[c, s]]))
-        for s in range(SHORT):
-            trm[s] = terms[s]
-        for i in range(SHORT, N_BLK * SHORT):
-            trm_out[i - SHORT] = terms[i]
-
-        def send_terms(s):
-            return [
-                remote(trm_out.at[(d - 1) * SHORT + s], trm.at[(4 - d) * SHORT + s],
-                       trm_send.at[stage, s, d - 1], trm_recv.at[stage, s, 3 - d], peers[d])
-                for d in (1, 3, 2)
-            ]
-
-        trm_copies = send_terms(0)
-        if stage == 0:
-            trm_copies += send_terms(1)
-
         acc_h[...] = jnp.zeros(acc_h.shape, F32)
         acc_l[...] = jnp.zeros(acc_l.shape, F32)
         acc_y[...] = jnp.zeros(acc_y.shape, F32)
@@ -387,7 +395,8 @@
             reduce1.pair()
 
         if stage == 0:
-            make_plan()
+            plan_copy.wait()
+            known[1].wait()
             loads[2].wait()
 
         def backward(i, carry):
@@ -443,10 +452,6 @@
             return c
 
         lax.fori_loop(0, brows // rows_at_once, forward, 0)
-        if stage == 1:
-            reduce1.across()
-            trm_copies += send_terms(1)
-
         for copy in fet_copies:
             copy.wait()
         terms = []
@@ -478,7 +483,7 @@
         x_y[pl.ds(256 if stage == 0 else 0, 256)] = y + y.T
         if stage == 1:
             reduce2.scatter()
-            reduce1.gather()
+            reduce1.across()
 
         for copy in trm_copies:
             copy.wait()
@@ -495,9 +500,8 @@
 
         if stage == 1:
             reduce2.across()
+            reduce1.gather()
         lax.fori_loop(0, brows // 4, finish, 0)
-        if stage == 1:
-            reduce1.regroup()
         for copy in rim_copies:
             copy.wait()
         for q in range(HB):
@@ -511,6 +515,7 @@
     copy2 = pltpu.make_async_copy(f0, image2, out_sem.at[1])
     copy2.start()
     reduce2.gather()
+    reduce1.regroup()
     reduce1.finish()
     reduce2.finish()
     copy1.wait()
@@ -571,7 +576,7 @@
             collective_id=0, has_side_effects=True, vmem_limit_bytes=VMEM_LIMIT
         ),
         name="krylov",
-    )(near_cols, short_rows, short_cols, near_cols.reshape(1, -1), field, diag, near, short)
+    )(near_cols, short_rows.T, short_cols.T, near_cols.reshape(1, -1), field, diag, near, short)
 
 
 def mm(a, b):

time: 118 us -> 111 us (0.941)
  Pallas kernels: 114 us -> 110 us
  local copies, waits for them, and re-layouts: 2.67 us -> 0 us
    pallas_call x1, Pallas kernels: 84.5 us -> 80.6 us  [krylov(): pl.pallas_call(krylov_kernel, out_shape=(jax.ShapeDtypeStruct(field.shape...]
    unnamed x2 -> x0, local copies, waits for them, and re-layouts: 2.67 us -> none
where the time goes in v4:
time: 111 us
  Pallas kernels  110 us (99%)
    pallas_call x1, Pallas kernels, krylov(): pl.pallas_call(krylov_kernel, out_shape=(jax.ShapeDtypeStruct(field.shape...  80.6 us
    pallas_call x1, Pallas kernels, tail(): pl.pallas_call(tail_kernel, out_shape=(jax.ShapeDtypeStruct(r0.shape, F32...  29.6 us

profile of v4, /device:TPU:1, one launch (start us, length us, event | category | flops | bytes accessed | tf_op | source)
XLA Modules:
  0.0 111.1 jit_solution(1317096189236638483)
XLA Ops:
  0.6 80.6 %krylov.1 = (f32[32,128,256]{2,1,0:T(8,128)}, f32[32,128,256]{2,1,0:T(8,128)}, f32[768,256]{1,0:T(8,128)}, f32[256,256]{1,0:T(8,128)}) custom-call(s32[96]{0:T(128)} %cols.1, s32[2,4]{1,0:T(2,128)} %bitcast.14, s32[2,4]{1,0:T(2,128)} %bitcast.15, s32[1,96]{1,0:T(1,128)} %bitcast.13, f32[32,128,256]{2,1,0:T(8,128)} %bitcast.8, f32[32,128]{1,0:T(8,128)} %bitcast.12, ...), custom_call_target="tpu_custom_call" | custom-call | tf_op jit(solution)/shard_map/krylov/pallas_call | solution.py:545
  81.3 29.6 %tail.1 = (f32[4096,256]{1,0:T(8,128)}, f32[4096,256]{1,0:T(8,128)}) custom-call(f32[768,256]{1,0:T(8,128)} %get-tuple-element.6.grams1, f32[256,256]{1,0:T(8,128)} %get-tuple-element.7.grams2, f32[4096,256]{1,0:T(8,128)} %r0.1, f32[4096,256]{1,0:T(8,128)} %bitcast.9, f32[4096,256]{1,0:T(8,128)} %bitcast.10), custom_call_target="tpu_custom_call" | custom-call | tf_op jit(solution)/shard_map/tail/pallas_call | solution.py:713

commit v5 on v4

--- a/solution.py
+++ b/solution.py
@@ -32,6 +32,28 @@
     return lax.dot_general(a, b, (((0,), (0,)), ((), ())), preferred_element_type=F32)
 
 
+def mm(a, b):
+    return jnp.dot(a, b, precision=HIGHEST, preferred_element_type=F32)
+
+
+def mm3(a, b):
+    return jnp.dot(a, b, precision=lax.Precision.HIGH, preferred_element_type=F32)
+
+
+def on_diagonal():
+    at = (256, 256)
+    return lax.broadcasted_iota(jnp.int32, at, 0) == lax.broadcasted_iota(jnp.int32, at, 1)
+
+
+def identity():
+    return jnp.where(on_diagonal(), 1.0, 0.0)
+
+
+def scales(m):
+    kept = jnp.where(on_diagonal(), m, 0.0)
+    return lax.rsqrt(jnp.sum(kept, axis=0, keepdims=True)), lax.rsqrt(jnp.sum(kept, axis=1, keepdims=True))
+
+
 def three(w, e):
     hi, lo = split(w)
     return dot(jnp.concatenate([hi, hi, lo], axis=1), jnp.concatenate([e, e[:128]], axis=0))
@@ -69,12 +91,13 @@
 
 def krylov_kernel(
     cols, srows, scols, cols_row, field, diag, near, short,
-    image, image2, grams1, grams2,
+    image, image2, grams1, grams3, grams2, inverse0,
     f0, f1, ext, wn, ws, dsp, seg, rseg, tseg, halo, rim_out, rim_in, trm_out, trm_0, trm_1, fet_out, fet_0, fet_1,
     tile, idx_in, idx_sm, keyrow, plan_v, plan, tplan_v, tplan, acc_h, acc_l, acc_y,
-    x1, pair1, half1, buf1, part1, zbuf1, mid1, x2, buf2, part2, zbuf2, mid2,
+    x1, buf1, part1, zbuf1, mid1, x2, buf2, part2, zbuf2, mid2,
+    x3, buf3, part3, zbuf3, mid3, work, along, down,
     load_sem, out_sem, idx_sem, idx_send, idx_recv, halo_send, halo_recv, trm_send, trm_recv,
-    fet_send, fet_recv, rim_send, rim_recv, pair_sem, red1_sem, zred1_sem, red2_sem, zred2_sem,
+    fet_send, fet_recv, rim_send, rim_recv, red1_sem, zred1_sem, red2_sem, zred2_sem, red3_sem, zred3_sem,
 ):
     brows = f0.shape[0]
     b = lax.axis_index("blk")
@@ -128,11 +151,6 @@
     plan_copy = pltpu.make_async_copy(plan_v, plan, idx_sem.at[0])
     plan_copy.start()
 
-    def spread_diag(r, c):
-        dsp[r] = jnp.broadcast_to(diag[pl.ds(r, 1), :], (128, 128)).T * 0.5
-        return c
-
-    lax.fori_loop(0, brows, spread_diag, 0)
     seg[0] = jnp.zeros(seg.shape[1:], F32)
     rseg[0] = jnp.zeros(rseg.shape[1:], F32)
     tseg[0] = jnp.zeros(tseg.shape[1:], F32)
@@ -208,87 +226,26 @@
         def finish(self):
             self.each(lambda i: self.share(i).wait())
 
-    class PairReduce:
-        def __init__(self, x, pair, half, buf, part, zbuf, mid, res, psems, sems, zsems):
-            self.x, self.pair_in, self.half, self.buf = x, pair, half, buf
-            self.part, self.zbuf, self.mid, self.res = part, zbuf, mid, res
-            self.psems, self.sems, self.zsems = psems, sems, zsems
-            self.core, self.plane, self.planes = lax.rem(g, 2), lax.div(g, 2), n_grp // 2
-            self.other = (b, self.plane * 2 + 1 - self.core)
-            self.half_rows = x.shape[0] // 2
-            self.rows = self.half_rows // self.planes
-
-        def halved(self, ref, core):
-            return ref.at[pl.ds(pl.multiple_of(core * self.half_rows, self.half_rows), self.half_rows)]
-
-        def each(self, act):
-            def step(i, c):
-                act(i)
-                return c
-
-            lax.fori_loop(1, self.planes, step, 0)
-
-        def spread(self, i):
-            t = lax.rem(self.plane + i, self.planes)
-            return pltpu.make_async_remote_copy(
-                src_ref=self.half.at[pl.ds(pl.multiple_of(t * self.rows, self.rows), self.rows)],
-                dst_ref=self.buf.at[self.planes - 1 - i],
-                send_sem=self.sems.at[0, i - 1], recv_sem=self.sems.at[1, self.planes - 1 - i],
-                device_id=(b, t * 2 + self.core), device_id_type=MESH,
-            )
-
-        def own_piece(self):
-            at = self.core * self.half_rows + self.plane * self.rows
-            return pl.ds(pl.multiple_of(at, self.rows), self.rows)
-
-        def share(self, i):
-            t = lax.rem(self.plane + i, self.planes)
-            return pltpu.make_async_remote_copy(
-                src_ref=self.mid, dst_ref=self.res.at[self.own_piece()],
-                send_sem=self.sems.at[2, i - 1], recv_sem=self.sems.at[3, self.planes - 1 - i],
-                device_id=(b, t * 2 + self.core), device_id_type=MESH,
-            )
-
-        def pair(self):
-            self.paired = remote(
-                self.halved(self.x, 1 - self.core), self.pair_in, self.psems.at[0], self.psems.at[1], self.other
-            )
-
-        def scatter(self):
-            self.paired.wait()
-            at = pl.multiple_of(self.core * self.half_rows, self.half_rows)
-            self.half[...] = self.x[pl.ds(at, self.half_rows)] + self.pair_in[...]
-            self.each(lambda i: self.spread(i).start())
-
-        def across(self):
-            self.each(lambda i: self.spread(i).wait())
-            total = self.half[pl.ds(pl.multiple_of(self.plane * self.rows, self.rows), self.rows)]
-            for i in range(self.planes - 1):
-                total += self.buf[i]
-            self.part[...] = total
-            self.copies = [
-                remote(self.part, self.zbuf.at[3 - d], self.zsems.at[0, d - 1], self.zsems.at[1, 3 - d], peers[d])
-                for d in range(1, N_BLK)
-            ]
-
-        def gather(self):
-            for copy in self.copies:
-                copy.wait()
-            total = sector_sum(self.part, self.zbuf)
-            self.mid[...] = total
-            self.res[self.own_piece()] = total
-            self.each(lambda i: self.share(i).start())
-
-        def regroup(self):
-            self.each(lambda i: self.share(i).wait())
-            mine = self.halved(self.res, self.core)
-            self.paired = remote(mine, mine, self.psems.at[2], self.psems.at[3], self.other)
-
-        def finish(self):
-            self.paired.wait()
-
-    reduce1 = PairReduce(x1, pair1, half1, buf1, part1, zbuf1, mid1, grams1, pair_sem, red1_sem, zred1_sem)
+    reduce1 = Reduce(x1, buf1, part1, zbuf1, mid1, grams1, red1_sem, zred1_sem)
+    reduce3 = Reduce(x3, buf3, part3, zbuf3, mid3, grams3, red3_sem, zred3_sem)
     reduce2 = Reduce(x2, buf2, part2, zbuf2, mid2, grams2, red2_sem, zred2_sem)
+
+    def start_inverse():
+        rr0 = grams1[pl.ds(0, 256)]
+        along[...], down[...] = scales(rr0)
+        scaled = rr0 * along[...] * down[...]
+        bound = jnp.max(jnp.sum(jnp.abs(scaled), axis=1, keepdims=True))
+        work[:256] = identity() / bound
+        work[256:] = identity() - scaled / bound
+
+    def double_inverse(times):
+        def step(i, c):
+            both = mm3(work[...], work[256:])
+            work[:256] = work[:256] + both[:256]
+            work[256:] = both[256:]
+            return c
+
+        lax.fori_loop(0, times, step, 0)
 
     per = 8
     back = 12
@@ -303,15 +260,18 @@
         wanted = [scols[s, b] for s in range(SHORT)]
         for d in range(1, N_BLK):
             wanted += [idx_sm[d - 1, b, s] for s in range(SHORT)]
+        return wanted
+
+    def order_wanted(wanted):
         tplan_v[...] = jnp.zeros(tplan_v.shape, jnp.int32)
         tplan_v[0:1, :], tplan_v[1:2, :], tplan_v[2:3, :] = order(lanes(wanted), 8)
         tplan_copy = pltpu.make_async_copy(tplan_v, tplan, idx_sem.at[2])
         tplan_copy.start()
-        return wanted, tplan_copy
+        return tplan_copy
 
     known = []
 
-    def operate(stage, fv, out, x_h, x_y, x_at, trm, fet):
+    def operate(stage, fv, out, x_h, x_y, trm, fet):
         if stage == 0:
             loads[0].wait()
         halo_copies = [
@@ -359,8 +319,17 @@
         trm_copies = send_terms(0)
         trm_copies += send_terms(1)
         if stage == 0:
-            known.extend(learn_wanted())
+            known.append(learn_wanted())
             fet_copies = send_fetch(known[0])
+            known.append(order_wanted(known[0]))
+
+            def spread_diag(i, c):
+                for u in range(8):
+                    r = i * 8 + u
+                    dsp[r] = jnp.broadcast_to(diag[pl.ds(r, 1), :], (128, 128)).T * 0.5
+                return c
+
+            lax.fori_loop(0, brows // 8, spread_diag, 0)
 
         def split_own(i, c):
             for u in range(4):
@@ -390,9 +359,12 @@
 
         lax.fori_loop(0, brows // per, gram, 0)
         low = acc_l[...]
-        x_h[pl.ds(x_at, 256)] = acc_h[...] + (low + low.T)
-        if stage == 1:
-            reduce1.pair()
+        x_h[pl.ds(256 * stage, 256)] = acc_h[...] + (low + low.T)
+        if stage == 0:
+            reduce1.scatter()
+        else:
+            reduce3.scatter()
+            reduce1.gather()
 
         if stage == 0:
             plan_copy.wait()
@@ -420,8 +392,6 @@
             remote(rim_out.at[pl.ds(HB, HB)], rim_in.at[stage, pl.ds(0, HB)],
                    rim_send.at[stage, 1], rim_recv.at[stage, 1], right),
         ]
-        if stage == 1:
-            reduce1.scatter()
 
         for copy in halo_copies:
             copy.wait()
@@ -480,10 +450,13 @@
 
         lax.fori_loop(0, brows // per, gram_y, 0)
         y = acc_y[...]
-        x_y[pl.ds(256 if stage == 0 else 0, 256)] = y + y.T
+        x_y[pl.ds(0, 256)] = y + y.T
         if stage == 1:
             reduce2.scatter()
-            reduce1.across()
+            reduce1.finish()
+            start_inverse()
+            reduce3.across()
+            double_inverse(6)
 
         for copy in trm_copies:
             copy.wait()
@@ -498,9 +471,12 @@
                 out[r] = (out[r] + half_diag(r)) + (seg[plan[LAST, HB + r]] + tseg[tplan[LAST, r]])
             return c
 
-        if stage == 1:
+        if stage == 0:
+            reduce1.across()
+        else:
             reduce2.across()
-            reduce1.gather()
+            reduce3.gather()
+            double_inverse(4)
         lax.fori_loop(0, brows // 4, finish, 0)
         for copy in rim_copies:
             copy.wait()
@@ -508,15 +484,16 @@
             out[q] = out[q] + rim_in[stage, q]
             out[brows - HB + q] = out[brows - HB + q] + rim_in[stage, HB + q]
 
-    operate(0, f0, f1, x1, x1, 0, trm_0, fet_0)
+    operate(0, f0, f1, x1, x3, trm_0, fet_0)
     copy1 = pltpu.make_async_copy(f1, image, out_sem.at[0])
     copy1.start()
-    operate(1, f1, f0, x1, x2, 512, trm_1, fet_1)
+    operate(1, f1, f0, x3, x2, trm_1, fet_1)
     copy2 = pltpu.make_async_copy(f0, image2, out_sem.at[1])
     copy2.start()
     reduce2.gather()
-    reduce1.regroup()
-    reduce1.finish()
+    double_inverse(4)
+    inverse0[...] = work[:256] * along[...] * down[...]
+    reduce3.finish()
     reduce2.finish()
     copy1.wait()
     copy2.wait()
@@ -547,11 +524,13 @@
         out_shape=(
             jax.ShapeDtypeStruct(field.shape, F32),
             jax.ShapeDtypeStruct(field.shape, F32),
-            jax.ShapeDtypeStruct((768, 256), F32),
+            jax.ShapeDtypeStruct((256, 256), F32),
+            jax.ShapeDtypeStruct((512, 256), F32),
+            jax.ShapeDtypeStruct((256, 256), F32),
             jax.ShapeDtypeStruct((256, 256), F32),
         ),
         in_specs=[smem, smem, smem, vmem, hbm, vmem, hbm, hbm],
-        out_specs=(hbm, hbm, vmem, vmem),
+        out_specs=(hbm, hbm, vmem, vmem, vmem, vmem),
         scratch_shapes=[
             block(brows), block(brows),
             pltpu.VMEM((brows + 2 * HB, 256, 256), BF16),
@@ -564,13 +543,14 @@
             words(), words(3), pltpu.SMEM((3, 8, 128), jnp.int32), words(),
             words(), pltpu.SMEM((8, 128), jnp.int32), words(), pltpu.SMEM((8, 128), jnp.int32),
             pltpu.VMEM((256, 256), F32), pltpu.VMEM((256, 256), F32), pltpu.VMEM((256, 256), F32),
-            pltpu.VMEM((768, 256), F32), pltpu.VMEM((384, 256), F32), pltpu.VMEM((384, 256), F32),
-            *reduce_scratch(16, 24),
             pltpu.VMEM((256, 256), F32), *reduce_scratch(32, 8),
+            pltpu.VMEM((256, 256), F32), *reduce_scratch(32, 8),
+            pltpu.VMEM((512, 256), F32), *reduce_scratch(32, 16),
+            pltpu.VMEM((512, 256), F32), pltpu.VMEM((1, 256), F32), pltpu.VMEM((256, 1), F32),
             dma((3,)), dma((2,)), dma((3,)), dma((3,)), dma((3,)),
             dma((2, 2)), dma((2, 2)), dma((2, 2, 3)), dma((2, 2, 3)), dma((2, 3)), dma((2, 3)),
             dma((2, 2)), dma((2, 2)),
-            dma((4,)), dma((4, n_grp // 2 - 1)), dma((2, 3)), dma((4, n_grp - 1)), dma((2, 3)),
+            dma((4, n_grp - 1)), dma((2, 3)), dma((4, n_grp - 1)), dma((2, 3)), dma((4, n_grp - 1)), dma((2, 3)),
         ],
         compiler_params=pltpu.CompilerParams(
             collective_id=0, has_side_effects=True, vmem_limit_bytes=VMEM_LIMIT
@@ -579,16 +559,8 @@
     )(near_cols, short_rows.T, short_cols.T, near_cols.reshape(1, -1), field, diag, near, short)
 
 
-def mm(a, b):
-    return jnp.dot(a, b, precision=HIGHEST, preferred_element_type=F32)
-
-
-def mm3(a, b):
-    return jnp.dot(a, b, precision=lax.Precision.HIGH, preferred_element_type=F32)
-
-
 def tail_kernel(
-    grams1, grams2, r0, q1, s2, sol, res,
+    grams1, grams3, grams2, inverse0, r0, q1, s2, sol, res,
     rv, qv, sv, sol_v, res_v, w_sol, w_res, work, load_sem, sol_sem, res_sem,
 ):
     loads = [
@@ -598,12 +570,8 @@
     for copy in loads:
         copy.start()
     n = 256
-    diagonal = lax.broadcasted_iota(jnp.int32, (n, n), 0) == lax.broadcasted_iota(jnp.int32, (n, n), 1)
-    eye = jnp.where(diagonal, 1.0, 0.0)
-
-    def scales(m):
-        kept = jnp.where(diagonal, m, 0.0)
-        return lax.rsqrt(jnp.sum(kept, axis=0, keepdims=True)), lax.rsqrt(jnp.sum(kept, axis=1, keepdims=True))
+    diagonal = on_diagonal()
+    eye = identity()
 
     def size(m):
         return jnp.max(jnp.abs(m))
@@ -640,19 +608,16 @@
             square(48)
             polish(scaled)
 
-        if guess is None:
+        near = guess / along / down
+        z = mm(scaled, near)
+        tau = n / jnp.sum(jnp.where(diagonal, z, 0.0))
+        work[:n, :] = near * tau
+        work[n:, :] = eye - z * tau
+        left = square(6)
+
+        @pl.when(jnp.logical_not(left <= 1e-5))
+        def _():
             from_norm()
-        else:
-            near = guess / along / down
-            z = mm(scaled, near)
-            tau = n / jnp.sum(jnp.where(diagonal, z, 0.0))
-            work[:n, :] = near * tau
-            work[n:, :] = eye - z * tau
-            left = square(6)
-
-            @pl.when(jnp.logical_not(left <= 1e-5))
-            def _():
-                from_norm()
 
         return work[:n, :] * along * down
 
@@ -660,9 +625,9 @@
         x = mm3(inverse, rhs)
         return x + mm3(inverse, rhs - mm(matrix, x))
 
-    rr0, g01, g11 = (grams1[i * n : (i + 1) * n, :] for i in range(3))
-    g12 = grams2[...]
-    inv0 = spd_inverse(rr0, None)
+    rr0, g12 = grams1[...], grams2[...]
+    g01, g11 = (grams3[i * n : (i + 1) * n, :] for i in range(2))
+    inv0 = spd_inverse(rr0, inverse0[...])
     a1 = solve(g01, spd_inverse(g01, inv0), rr0)
     ga = mm(g01, a1)
     g11a = mm(g11, a1)
@@ -705,7 +670,7 @@
         pltpu.make_async_copy(res_v.at[at], res.at[at], res_sem.at[i]).wait()
 
 
-def tail(grams1, grams2, r0, q1, s2):
+def tail(grams1, grams3, grams2, inverse0, r0, q1, s2):
     vmem = pl.BlockSpec(memory_space=pltpu.VMEM)
     hbm = pl.BlockSpec(memory_space=pl.ANY)
     dma = pltpu.SemaphoreType.DMA
@@ -713,7 +678,7 @@
     return pl.pallas_call(
         tail_kernel,
         out_shape=(jax.ShapeDtypeStruct(r0.shape, F32),) * 2,
-        in_specs=[vmem, vmem, hbm, hbm, hbm],
+        in_specs=[vmem, vmem, vmem, vmem, hbm, hbm, hbm],
         out_specs=(hbm, hbm),
         scratch_shapes=[
             field, field, field, field, field,
@@ -723,17 +688,17 @@
         ],
         compiler_params=pltpu.CompilerParams(vmem_limit_bytes=VMEM_LIMIT),
         name="tail",
-    )(grams1, grams2, r0, q1, s2)
+    )(grams1, grams3, grams2, inverse0, r0, q1, s2)
 
 
 def body(loads, pore_diag, near_blocks, near_cols, short_blocks, short_rows, short_cols):
     rows, cases = loads.shape
     brows = rows // 128
-    q1, s2, grams1, grams2 = krylov(
+    q1, s2, grams1, grams3, grams2, inverse0 = krylov(
         near_cols, short_rows, short_cols, loads.reshape(brows, 128, cases), pore_diag.reshape(brows, 128),
         near_blocks, short_blocks.reshape(-1, 128, 128),
     )
-    return tail(grams1, grams2, loads, q1.reshape(rows, cases), s2.reshape(rows, cases))
+    return tail(grams1, grams3, grams2, inverse0, loads, q1.reshape(rows, cases), s2.reshape(rows, cases))
 
 
 def solution(mesh):

time: 111 us -> 109 us (0.982)
  Pallas kernels: 110 us -> 108 us
    pallas_call x1, Pallas kernels: 29.6 us -> 21.9 us  [tail(): pl.pallas_call(tail_kernel, out_shape=(jax.ShapeDtypeStruct(r0.shape, F32...]
    pallas_call x1, Pallas kernels: 80.6 us -> 85.8 us  [krylov(): pl.pallas_call(krylov_kernel, out_shape=(jax.ShapeDtypeStruct(field.shape...]
where the time goes in v5:
time: 109 us
  Pallas kernels  108 us (99%)
    pallas_call x1, Pallas kernels, krylov(): pl.pallas_call(krylov_kernel, out_shape=(jax.ShapeDtypeStruct(field.shape...  85.8 us
    pallas_call x1, Pallas kernels, tail(): pl.pallas_call(tail_kernel, out_shape=(jax.ShapeDtypeStruct(r0.shape, F32...  21.9 us

profile of v5, /device:TPU:1, one launch (start us, length us, event | category | flops | bytes accessed | tf_op | source)
XLA Modules:
  0.0 108.6 jit_solution(2098274645105356211)
XLA Ops:
  0.6 85.8 %krylov.1 = (f32[32,128,256]{2,1,0:T(8,128)}, f32[32,128,256]{2,1,0:T(8,128)}, f32[256,256]{1,0:T(8,128)}, f32[512,256]{1,0:T(8,128)}, f32[256,256]{1,0:T(8,128)}, /*index=5*/f32[256,256]{1,0:T(8,128)}) custom-call(s32[96]{0:T(128)} %cols.1, s32[2,4]{1,0:T(2,128)} %bitcast.14, s32[2,4]{1,0:T(2,128)} %bitcast.15, s32[1,96]{1,0:T(1,128)} %bitcast.13, ...), custom_call_target="tpu_custom_call" | custom-call | tf_op jit(solution)/shard_map/krylov/pallas_call | solution.py:522
  86.5 21.9 %tail.1 = (f32[4096,256]{1,0:T(8,128)}, f32[4096,256]{1,0:T(8,128)}) custom-call(f32[256,256]{1,0:T(8,128)} %get-tuple-element.8.grams1, f32[512,256]{1,0:T(8,128)} %get-tuple-element.9.grams3, f32[256,256]{1,0:T(8,128)} %get-tuple-element.10.grams2, f32[256,256]{1,0:T(8,128)} %get-tuple-element.11.inverse0, f32[4096,256]{1,0:T(8,128)} %r0.1, ...), custom_call_target="tpu_custom_call" | custom-call | tf_op jit(solution)/shard_map/tail/pallas_call | solution.py:678
